TPU v7x, 256 devices: a whole 4x4x8 slice. The times are simulated.
256 devices in a mesh: row: 8 (over z), col: 8 (over x, core), depth: 4 (over y).
Axes of the slice: x: 4, y: 4, z: 8, core: 2. Of those that a mesh axis runs over, the one named last changes fastest.
Arguments:
- amplitudes: bfloat16 [6400, 7200], P('row', ('col', 'depth')), may hold values from -6 to 6
- integrals: bfloat16 [7200, 16384], P('row', ('col', 'depth')), may hold values from -0.0625 to 0.0625
- cycle_integrals: bfloat16 [512, 512], P('row'), as said below
- occ_irrep: int32 [100], replicated, may hold values from 0 to 7
- vir_irrep: int32 [900], replicated, may hold values from 0 to 7
Outputs:
- ladder: bfloat16 [6400, 16384], P('row', ('col', 'depth'))
- cycle: bfloat16 [512, 57600], P('row', ('col', 'depth'))
Inputs may be any that keep to these rules, and one draw needn't show every extreme that they name: cycle_integrals equals its transpose.
All inputs are finite; a program needn't handle non-finite values.
Results may differ from a plain program's by a relative error of at most 0.001.
Values may be sent and summed in bfloat16 or wider, within the bound.
No kernel may reach another device: no remote copies, remote signals or barrier semaphores. Data moves between devices by JAX's collectives and lax.ppermute only.
A program may use at most 128 MiB of HBM per device.

v0:
```python
import jax
import jax.numpy as jnp
from jax import lax
from jax.sharding import PartitionSpec as P

NO = 100
NV = 900
JW = 64
CW = 8


def label_bits(labels):
    return jnp.stack([labels % 2, labels // 2 % 2, labels // 4 % 2])


def lookup(lookup_table, indices):
    matches = indices[:, None] == jnp.arange(lookup_table.shape[0], dtype=jnp.int32)[None, :]
    return jnp.sum(jnp.where(matches, lookup_table[None, :], 0), axis=1)


def shards(amplitudes, integrals, cycle_integrals, occ_irrep, vir_irrep):
    rows_here = amplitudes.shape[0]
    occ_block = rows_here // NO
    local_cols = amplitudes.shape[1]
    regroup_in = amplitudes.reshape(occ_block, NO, local_cols)[:, :JW, :]
    spread = lax.all_to_all(regroup_in, ("col", "depth"), split_axis=1, concat_axis=2, tiled=True)
    occ_here = spread.shape[1]
    ordered = (
        spread.reshape(occ_block, occ_here, CW, NV)
        .transpose(0, 2, 1, 3)
        .reshape(occ_block * CW, occ_here * NV)
    )
    columns = occ_here * NV
    integ_all = lax.all_gather(integrals, "row", axis=0, tiled=True)
    ladder_sum = jnp.dot(
        lax.all_gather(amplitudes, ("col", "depth"), axis=1, tiled=True),
        integ_all,
        preferred_element_type=jnp.float32,
    )
    ladder = ladder_sum.astype(jnp.bfloat16)
    cycle_rows_here = cycle_integrals.shape[0]
    cycle_sum = jnp.dot(
        cycle_integrals,
        lax.all_gather(ordered, "row", axis=0, tiled=True),
        preferred_element_type=jnp.float32,
    )
    occ_bits = label_bits(occ_irrep)
    vir_bits = label_bits(vir_irrep)
    row_ids = lax.axis_index("row") * cycle_rows_here + jnp.arange(cycle_rows_here, dtype=jnp.int32)
    column_ids = lax.axis_index(("col", "depth")) * columns + jnp.arange(columns, dtype=jnp.int32)
    occ_first = row_ids // CW
    virt_first = row_ids % CW
    occ_second = column_ids // NV
    virt_second = column_ids % NV
    odd_count = jnp.zeros((cycle_rows_here, columns), jnp.int32)
    for digit in range(3):
        row_bits = lookup(occ_bits[digit], occ_first) + lookup(vir_bits[digit], virt_first)
        column_bits = lookup(occ_bits[digit], occ_second) + lookup(vir_bits[digit], virt_second)
        odd_count = odd_count + (row_bits[:, None] + column_bits[None, :]) % 2
    cycle = jnp.where(odd_count == 0, cycle_sum, jnp.float32(0.0)).astype(jnp.bfloat16)
    return (ladder, cycle)


def solution(mesh):
    in_specs = (P("row", ("col", "depth")), P("row", ("col", "depth")), P("row", None), P(), P())
    out_specs = (P("row", ("col", "depth")), P("row", ("col", "depth")))
    return jax.shard_map(shards, mesh=mesh, in_specs=in_specs, out_specs=out_specs, check_vma=False)
```

profile of v0, /device:TPU:2, one launch (start us, length us, event | category | flops | bytes accessed | tf_op | source)
XLA Modules:
  0.0 285.9 jit_solution(8054092691245306198)
XLA Ops:
  7.2 0.0 copy-start
  7.2 0.0 all-gather.6.cloned.1.call-start
  7.2 1.1 reshape.100
  8.4 0.2 copy.15
  8.5 15.3 %all_to_all.15 = bf16[8,64,225]{2,0,1:T(8,128)(2,1)S(1)} all-to-all(bf16[8,64,225]{2,0,1:T(8,128)(2,1)S(1)} %copy.15), channel_id=1, replica_groups=mesh['row'=8,'col'=8,'depth'=4] {'col','depth'}, dimensions={1} | all-to-all | bytes 460800 | tf_op jit(solution)/shard_map/all_to_all | solution.py:26
  23.8 0.1 copy.19
  23.9 0.4 reshape.101
  24.3 0.3 copy.17
  24.6 0.9 reshape.102
  25.5 0.0 all-gather.6.cloned.1.call-update
  25.6 0.0 all-gather.10.cloned.1.call-start
  25.6 0.7 all-gather.10.cloned.1.call-update
  26.3 0.0 all-gather.8.cloned.1.call-start
  26.4 0.7 all-gather.8.cloned.1.call-update
  27.1 0.7 and_select_fusion.2
  27.8 0.4 select_reduce_fusion.5
  28.1 0.7 add_select_fusion.10
  28.9 2.9 %select_reduce_fusion.2 = (s32[1800]{0:T(1024)S(1)}, s32[1800]{0:T(1024)S(1)}, s32[1800]{0:T(1024)S(1)}) fusion(s32[900]{0:T(1024)S(1)} %get-tuple-element.16, s32[1800]{0:T(1024)S(1)} %get-tuple-element.20, s32[900]{0:T(1024)S(1)} %get-tuple-element.15, s32[900]{0:T(1024)S(1)} %get-tuple-element.14), kind=kLoop, calls=%fused_computation.2 | loop fusion | flops 11334600 | bytes 39600 | tf_op jit(solution)/shard_map/reduce_sum | solution.py:18
  31.8 0.2 select_reduce_fusion.11
  32.0 0.3 select_reduce_fusion.8
  32.3 34.5 %all-gather.6.cloned.1.call-done = bf16[512,1800]{1,0:T(8,128)(2,1)} async-done(((bf16[64,1800]{1,0:T(8,128)(2,1)}), bf16[512,1800]{1,0:T(8,128)(2,1)}) %all-gather.6.cloned.1.call-update) | async-done | bytes 1843216 | tf_op jit(solution)/shard_map/all_gather | solution.py:44
  66.9 0.0 copy-done
  66.9 3.1 %fusion = bf16[64,1800]{1,0:T(8,128)(2,1)} fusion(bf16[64,512]{1,0:T(8,128)(2,1)S(1)} %copy-done, bf16[512,1800]{1,0:T(8,128)(2,1)} %all-gather.6.cloned.1.call-done, s32[1800]{0:T(1024)S(1)} %add.220, s32[64]{0:T(128)S(1)} %add.218, s32[1800]{0:T(1024)S(1)} %add.211, s32[64]{0:T(128)S(1)} %add.209, s32[1800]{0:T(1024)S(1)} %add.203, s32[64]{0:T(128)S(1)} %add.197), kind=kOutput, calls=%fused_computation.5 | convolution fusion | flops 122688000 | bytes 2161504 | tf_op jit(solution)/shard_map/dot_general | solution.py:42
  70.0 82.3 %all-gather.10.cloned.1.call-done = bf16[8,900,512]{2,1,0:T(8,128)(2,1)} async-done(((bf16[1,900,512]{2,1,0:T(8,128)(2,1)}), bf16[8,900,512]{2,1,0:T(8,128)(2,1)}) %all-gather.10.cloned.1.call-update) | async-done | bytes 7372816 | tf_op jit(solution)/shard_map/all_gather | solution.py:34
  152.3 6.9 %reshape.106 = bf16[7200,512]{1,0:T(8,128)(2,1)} reshape(bf16[8,900,512]{2,1,0:T(8,128)(2,1)} %all-gather.10.cloned.1.call-done) | data formatting | bytes 14745600
  159.2 63.3 %all-gather.8.cloned.1.call-done = bf16[32,225,800]{1,2,0:T(8,128)(2,1)} async-done(((bf16[1,225,800]{1,2,0:T(8,128)(2,1)}), bf16[32,225,800]{1,2,0:T(8,128)(2,1)}) %all-gather.8.cloned.1.call-update) | async-done | bytes 11520016 | tf_op jit(solution)/shard_map/all_gather | solution.py:36
  222.5 20.2 %copy.14 = bf16[32,225,800]{1,0,2:T(8,128)(2,1)} copy(bf16[32,225,800]{1,2,0:T(8,128)(2,1)} %all-gather.8.cloned.1.call-done) | data formatting | bytes 23040000 | tf_op jit(solution)/shard_map/all_gather | solution.py:36
  242.8 24.6 %reshape.104 = bf16[7200,800]{0,1:T(8,128)(2,1)} reshape(bf16[32,225,800]{1,0,2:T(8,128)(2,1)} %copy.14) | data formatting | bytes 23040000
  267.4 12.0 %convolution_convert_fusion = bf16[800,512]{1,0:T(8,128)(2,1)} fusion(bf16[7200,800]{0,1:T(8,128)(2,1)} %reshape.104, bf16[7200,512]{1,0:T(8,128)(2,1)} %reshape.106), kind=kOutput, calls=%fused_computation.6 | convolution fusion | flops 5898649600 | bytes 19712000 | tf_op jit(solution)/shard_map/dot_general | solution.py:35
  (9 shorter events, 0.1 us)
Async XLA Ops:
  7.2 59.7 %copy-start = (bf16[64,512]{1,0:T(8,128)(2,1)S(1)}, bf16[64,512]{1,0:T(8,128)(2,1)}, u32[]{:S(2)}) copy-start(bf16[64,512]{1,0:T(8,128)(2,1)} %param.7) | copy-start | bytes 196612
  7.2 59.7 %all-gather.6.cloned.1.call-start = ((), (), s32[]{:S(2)}) async-start(), calls=%async_computation.1 | async-start | bytes 2211840 | tf_op jit(solution)/shard_map/all_gather | solution.py:44
  25.6 126.7 %all-gather.10.cloned.1.call-start = ((), (), s32[]{:S(2)}) async-start(), calls=%async_computation.3 | async-start | bytes 8331264 | tf_op jit(solution)/shard_map/all_gather | solution.py:34
  26.3 196.2 %all-gather.8.cloned.1.call-start = ((), (), s32[]{:S(2)}) async-start(), calls=%async_computation.2 | async-start | bytes 13516800 | tf_op jit(solution)/shard_map/all_gather | solution.py:36
Sparse Core Ops, SparseCore 0:
  25.7 41.1 all-gather.5
  68.6 83.6 all-gather.9
  154.9 67.5 all-gather.7
where the time goes:
time: 288 us; the launch traced here: 286 us
  waiting for transfers between devices  182 us (63%)
  local copies, waits for them, and re-layouts  54.7 us (19%)
  blocking collectives  15.3 us (5%)
  matrix products  15.2 us (5%)
  between operations  13.9 us (5%)
  other arithmetic  5.2 us (2%)
    all_gather x1, waiting for transfers between devices, shards(): integ_all = lax.all_gather(integrals, 'row', axis=0, tiled=True)  82.3 us
    all_gather x1, waiting for transfers between devices, shards(): lax.all_gather(amplitudes, ('col', 'depth'), axis=1, tiled=True)  63.3 us
    all_gather x1, waiting for transfers between devices, shards(): lax.all_gather(ordered, 'row', axis=0, tiled=True)  34.5 us
    unnamed x4, local copies, waits for them, and re-layouts  31.5 us
    all_gather x1, local copies, waits for them, and re-layouts, shards(): lax.all_gather(amplitudes, ('col', 'depth'), axis=1, tiled=True)  20.2 us
    all_to_all x1, blocking collectives, shards(): lax.all_to_all(regroup_in, ('col', 'depth'), split_axis=1, concat_axis=2,...  15.3 us
    dot_general x1, matrix products, shards(): jnp.dot(lax.all_gather(amplitudes, ('col', 'depth'), axis=1, tiled=True),...  12 us
  transfers between devices with their start and end apart: 3, of which 3 were waited for; matrix products, arithmetic and copies ran while one was open for 5% of the time, Pallas kernels for 0%

commit v1 on v0

v1 whole, which is shorter than its diff:
```python
import functools

import jax
import jax.numpy as jnp
from jax import lax
from jax.experimental import pallas as pl
from jax.experimental.pallas import tpu as pltpu
from jax.sharding import PartitionSpec as P

NO = 100
NV = 900
JW = 64
CW = 8
RING = 8
QUARTERS = 4
UP = [(i, (i + 1) % RING) for i in range(RING)]
DOWN = [(i, (i - 1) % RING) for i in range(RING)]


def shift(value, step):
    return lax.ppermute(value, "row", UP if step > 0 else DOWN)


def ladder_kernel(n, first, last, owner_ref, amps_ref, *refs):
    blocks = refs[: 2 * n]
    refs = refs[2 * n :]
    before_ref = None
    if not first:
        before_ref, refs = refs[0], refs[1:]
    out_ref, held, sems = refs[0], refs[1], refs[2]
    total = refs[3] if last and n > 1 else out_ref

    def fetch(k):
        start = pl.multiple_of(owner_ref[k] * QUARTERS, QUARTERS)
        return pltpu.make_async_copy(
            amps_ref.at[pl.ds(start, QUARTERS)], held.at[k % 2], sems.at[k % 2]
        )

    fetch(0).start()
    for k in range(n):
        fetch(k).wait()
        if k + 1 < n:
            fetch(k + 1).start()

        def tile(m, _, k=k):
            rows = pl.ds(pl.multiple_of(m * 400, 400), 400)
            value = None
            for q in range(QUARTERS):
                term = jnp.dot(
                    held[k % 2, q, rows, :],
                    blocks[2 * k + q // 2][q % 2],
                    preferred_element_type=jnp.float32,
                )
                value = term if value is None else value + term
            if k > 0:
                value = value + total[rows, :]
            elif before_ref is not None:
                value = value + before_ref[rows, :]
            if last and k == n - 1:
                out_ref[rows, :] = value.astype(out_ref.dtype)
            else:
                total[rows, :] = value
            return 0

        lax.fori_loop(0, 2, tile, 0)


def ladder_part(owners, amps, blocks, before, last):
    n = len(blocks) // 2
    rows, columns = amps.shape[1], blocks[0].shape[2]
    first = before is None
    scratch = [
        pltpu.VMEM((2, QUARTERS) + amps.shape[1:], jnp.bfloat16),
        pltpu.SemaphoreType.DMA((2,)),
    ]
    if last and n > 1:
        scratch.append(pltpu.VMEM((rows, columns), jnp.float32))
    whole = pl.BlockSpec(memory_space=pltpu.VMEM)
    return pl.pallas_call(
        functools.partial(ladder_kernel, n, first, last),
        out_shape=jax.ShapeDtypeStruct((rows, columns), jnp.bfloat16 if last else jnp.float32),
        in_specs=[pl.BlockSpec(memory_space=pltpu.SMEM), pl.BlockSpec(memory_space=pl.ANY)]
        + [whole] * (2 * n + (0 if first else 1)),
        out_specs=whole,
        scratch_shapes=scratch,
        compiler_params=pltpu.CompilerParams(vmem_limit_bytes=40 << 20),
        cost_estimate=pl.CostEstimate(
            flops=2 * rows * NV * columns * n,
            bytes_accessed=2 * n * NV * (rows + columns),
            transcendentals=0,
        ),
    )(owners, amps, *blocks, *([] if first else [before]))


def shards(amplitudes, integrals, cycle_integrals, occ_irrep, vir_irrep):
    rows_here, local_cols = amplitudes.shape
    occ_block = rows_here // NO
    z = lax.axis_index("row")
    p = lax.axis_index(("col", "depth"))

    gathered = lax.all_gather(amplitudes, ("col", "depth"), axis=0, tiled=True)
    gathered = gathered.reshape(RING * QUARTERS, rows_here, local_cols)

    half = NV // 2
    top = integrals[:half].reshape(2, half // 2, -1)
    bot = integrals[half:].reshape(2, half // 2, -1)

    regroup_in = amplitudes.reshape(occ_block, NO, local_cols)[:, :JW, :]
    spread = lax.all_to_all(regroup_in, ("col", "depth"), split_axis=1, concat_axis=2, tiled=True)
    occ_here = spread.shape[1]
    columns = occ_here * NV
    ordered = (
        spread.reshape(occ_block, occ_here, CW, NV)
        .transpose(0, 2, 1, 3)
        .reshape(occ_block * CW, columns)
    )

    tops, bots, regrouped = {0: top}, {0: bot}, {0: ordered}
    for s in range(1, 5):
        tops[-s] = shift(tops[1 - s], 1)
        bots[s] = shift(bots[s - 1], -1)
        if s < 4:
            bots[-s] = shift(bots[1 - s], 1)
            tops[s] = shift(tops[s - 1], -1)
            regrouped[-s] = shift(regrouped[1 - s], 1)
            regrouped[s] = shift(regrouped[s - 1], -1)
    tops[4] = tops.pop(-4)
    width = ordered.shape[0] // 2
    regrouped[4] = jnp.concatenate(
        [shift(regrouped[-3][:width], 1), shift(regrouped[3][width:], -1)], axis=0
    )

    def blocks(offsets):
        return [b for d in offsets for b in (tops[d], bots[d])]

    def owners(offsets):
        return jnp.stack([(z + d) % RING for d in offsets]).astype(jnp.int32)

    early, late = [0, -1, 1, -2, 2, -3, 3], [4]
    total = ladder_part(owners(early), gathered, blocks(early), None, False)
    ladder = ladder_part(owners(late), gathered, blocks(late), total, True)

    rel = list(range(RING))
    stacked = jnp.concatenate([regrouped[d if d <= 4 else d - RING] for d in rel], axis=0)
    per_row = cycle_integrals.shape[1] // RING
    twice = jnp.concatenate([cycle_integrals, cycle_integrals], axis=1)
    rolled = lax.dynamic_slice_in_dim(twice, z * per_row, RING * per_row, axis=1)
    cycle_sum = jnp.dot(rolled, stacked, preferred_element_type=jnp.float32)

    rows_cycle = cycle_integrals.shape[0]
    occ_rows = lax.dynamic_slice_in_dim(occ_irrep, z * (rows_cycle // CW), rows_cycle // CW)
    row_label = ((occ_rows[:, None] ^ vir_irrep[None, :CW]) & 7).reshape(rows_cycle)
    occ_cols = lax.dynamic_slice_in_dim(occ_irrep, p * occ_here, occ_here)
    col_label = ((occ_cols[:, None] ^ vir_irrep[None, :]) & 7).reshape(columns)
    allowed = row_label[:, None] == col_label[None, :]
    cycle = jnp.where(allowed, cycle_sum, jnp.float32(0.0)).astype(jnp.bfloat16)
    return ladder, cycle


def solution(mesh):
    in_specs = (P("row", ("col", "depth")), P("row", ("col", "depth")), P("row", None), P(), P())
    out_specs = (P("row", ("col", "depth")), P("row", ("col", "depth")))
    return jax.shard_map(shards, mesh=mesh, in_specs=in_specs, out_specs=out_specs, check_vma=False)
```

time: 288 us -> 147 us (0.51)
  waiting for transfers between devices: 182 us -> 56.3 us
  starting transfers between devices: 0.12 us -> 44.5 us
  local copies, waits for them, and re-layouts: 54.7 us -> 12.7 us
  Pallas kernels: 0 us -> 17 us
  blocking collectives: 15.3 us -> 0 us
  matrix products: 15.2 us -> 1.25 us
  other arithmetic: 5.2 us -> 0.15 us
    all_gather x3 -> x1, waiting for transfers between devices: 180 us -> 0.01 us  [shards(): gathered = lax.all_gather(amplitudes, ('col', 'depth'), axis=0, tiled=True)]
    ppermute x0 -> x22, waiting for transfers between devices: none -> 47.5 us  [shift(): return lax.ppermute(value, 'row', UP if step > 0 else DOWN)]
    ppermute x0 -> x22, starting transfers between devices: none -> 36.8 us  [shift(): return lax.ppermute(value, 'row', UP if step > 0 else DOWN)]
    unnamed x4 -> x36, local copies, waits for them, and re-layouts: 31.5 us -> 7.83 us
    all_gather x1 -> x0, local copies, waits for them, and re-layouts: 20.2 us -> none  [shards(): lax.all_gather(amplitudes, ('col', 'depth'), axis=1, tiled=True)]
    pallas_call x0 -> x2, Pallas kernels: none -> 17 us  [ladder_part(): pl.pallas_call(functools.partial(ladder_kernel, n, first, last), out_shap...]
    all_to_all x1 -> x0, blocking collectives: 15.3 us -> none  [shards(): lax.all_to_all(regroup_in, ('col', 'depth'), split_axis=1, concat_axis=2,...]
    dot_general x2 -> x1, matrix products: 15.2 us -> 1.25 us  [shards(): cycle_sum = jnp.dot(rolled, stacked, preferred_element_type=jnp.float32)]
  transfers between devices with their start and end apart: 3 -> 24, of which waited for: 3 -> 8; matrix products, arithmetic and copies ran while one was open for 5% -> 5% of each run, Pallas kernels for 0% -> 8%
where the time goes in v1:
time: 147 us; the launch traced here: 146 us
  waiting for transfers between devices  56.3 us (38%)
  starting transfers between devices  44.5 us (30%)
  Pallas kernels  17 us (12%)
  between operations  14.4 us (10%)
  local copies, waits for them, and re-layouts  12.7 us (9%)
    ppermute x22, waiting for transfers between devices, shift(): return lax.ppermute(value, 'row', UP if step > 0 else DOWN)  47.5 us
    ppermute x22, starting transfers between devices, shift(): return lax.ppermute(value, 'row', UP if step > 0 else DOWN)  36.8 us
    pallas_call x2, Pallas kernels, ladder_part(): pl.pallas_call(functools.partial(ladder_kernel, n, first, last), out_shap...  17 us
    all_to_all x1, waiting for transfers between devices, shards(): lax.all_to_all(regroup_in, ('col', 'depth'), split_axis=1, concat_axis=2,...  8.1 us
    unnamed x36, local copies, waits for them, and re-layouts  7.83 us
    all_to_all x1, starting transfers between devices, shards(): lax.all_to_all(regroup_in, ('col', 'depth'), split_axis=1, concat_axis=2,...  7.62 us
  transfers between devices with their start and end apart: 24, of which 8 were waited for; matrix products, arithmetic and copies ran while one was open for 5% of the time, Pallas kernels for 8%

profile of v1, /device:TPU:2, one launch (start us, length us, event | category | flops | bytes accessed | tf_op | source)
XLA Modules:
  0.0 146.2 jit_solution(15390338617429027131)
XLA Ops:
  7.9 1.3 fusion.5
  9.4 5.9 %collective-permute-start.4 = (bf16[2,225,512]{2,1,0:T(8,128)(2,1)S(1)}, bf16[2,225,512]{2,1,0:T(8,128)(2,1)S(1)}, u32[]{:S(2)}, u32[]{:S(2)}) collective-permute-start(bf16[2,225,512]{2,1,0:T(8,128)(2,1)S(1)} %reshape.63.refs_1_), channel_id=1, source_target_pairs={{0,224},{32,0},{64,32},{96,64},{128,96},{160,128},{192,160},{224,1... | collective-permute-start | bytes 1382408 | tf_op jit(solution)/shard_map/ppermute | solution.py:21
  15.6 0.9 copy.9
  16.5 7.6 %all-to-all-start = ((bf16[8,64,225]{2,0,1:T(8,128)(2,1)}), bf16[8,64,225]{2,0,1:T(8,128)(2,1)S(1)}, u32[]{:S(2)}, u32[]{:S(2)}) async-start(bf16[8,64,225]{2,0,1:T(8,128)(2,1)} %copy.9), calls=%async_computation | async-start | bytes 524288 | tf_op jit(solution)/shard_map/all_to_all | solution.py:109
  24.3 8.1 %all-to-all-done = bf16[8,64,225]{2,0,1:T(8,128)(2,1)S(1)} async-done(((bf16[8,64,225]{2,0,1:T(8,128)(2,1)}), bf16[8,64,225]{2,0,1:T(8,128)(2,1)S(1)}, u32[]{:S(2)}, u32[]{:S(2)}) %all-to-all-start) | async-done | bytes 230432 | tf_op jit(solution)/shard_map/all_to_all | solution.py:109
  33.4 3.1 %collective-permute-start.14 = (bf16[64,1800]{1,0:T(8,128)(2,1)S(1)}, bf16[64,1800]{1,0:T(8,128)(2,1)}, u32[]{:S(2)}, u32[]{:S(2)}) collective-permute-start(bf16[64,1800]{1,0:T(8,128)(2,1)S(1)} %reshape.66), channel_id=1, source_target_pairs={{0,224},{32,0},{64,32},{96,64},{128,96},{160,128},{192,160},{224,1... | collective-permute-start | bytes 691208 | tf_op jit(solution)/shard_map/ppermute | solution.py:21
  36.9 5.2 %collective-permute-done.14 = bf16[64,1800]{1,0:T(8,128)(2,1)} collective-permute-done((bf16[64,1800]{1,0:T(8,128)(2,1)S(1)}, bf16[64,1800]{1,0:T(8,128)(2,1)}, u32[]{:S(2)}, u32[]{:S(2)}) %collective-permute-start.14) | collective-permute-done | bytes 230432 | tf_op jit(solution)/shard_map/ppermute | solution.py:21
  42.2 3.8 %collective-permute-start.9 = (bf16[2,225,512]{2,1,0:T(8,128)(2,1)S(1)}, bf16[2,225,512]{2,1,0:T(8,128)(2,1)S(1)}, u32[]{:S(2)}, u32[]{:S(2)}) collective-permute-start(bf16[2,225,512]{2,1,0:T(8,128)(2,1)S(1)} %reshape.62.refs_0_), channel_id=1, source_target_pairs={{0,224},{32,0},{64,32},{96,64},{128,96},{160,128},{192,160},{224,1... | collective-permute-start | bytes 1382408 | tf_op jit(solution)/shard_map/ppermute | solution.py:21
  46.0 3.3 %collective-permute-start.15 = (bf16[64,1800]{1,0:T(8,128)(2,1)}, bf16[64,1800]{1,0:T(8,128)(2,1)S(1)}, u32[]{:S(2)}, u32[]{:S(2)}) collective-permute-start(bf16[64,1800]{1,0:T(8,128)(2,1)} %collective-permute-done.14), channel_id=1, source_target_pairs={{0,224},{32,0},{64,32},{96,64},{128,96},{160,128},{192,160},{224,1... | collective-permute-start | bytes 691208 | tf_op jit(solution)/shard_map/ppermute | solution.py:21
  49.3 5.1 %collective-permute-done.18 = bf16[64,1800]{1,0:T(8,128)(2,1)S(1)} collective-permute-done((bf16[64,1800]{1,0:T(8,128)(2,1)}, bf16[64,1800]{1,0:T(8,128)(2,1)S(1)}, u32[]{:S(2)}, u32[]{:S(2)}) %collective-permute-start.18) | collective-permute-done | bytes 230432 | tf_op jit(solution)/shard_map/ppermute | solution.py:21
  54.4 1.0 constant_dynamic-update-slice_fusion.7
  55.5 3.3 %collective-permute-start.5 = (bf16[2,225,512]{2,1,0:T(8,128)(2,1)S(1)}, bf16[2,225,512]{2,1,0:T(8,128)(2,1)S(1)}, u32[]{:S(2)}, u32[]{:S(2)}) collective-permute-start(bf16[2,225,512]{2,1,0:T(8,128)(2,1)S(1)} %collective-permute-done.4.refs_5_), channel_id=1, source_target_pairs={{0,224},{32,0},{64,32},{96,64},{128,96},{160,128},{192,160},{224,1... | collective-permute-start | bytes 1382408 | tf_op jit(solution)/shard_map/ppermute | solution.py:21
  58.8 3.8 %collective-permute-done.15 = bf16[64,1800]{1,0:T(8,128)(2,1)S(1)} collective-permute-done((bf16[64,1800]{1,0:T(8,128)(2,1)}, bf16[64,1800]{1,0:T(8,128)(2,1)S(1)}, u32[]{:S(2)}, u32[]{:S(2)}) %collective-permute-start.15) | collective-permute-done | bytes 230432 | tf_op jit(solution)/shard_map/ppermute | solution.py:21
  62.6 3.6 %collective-permute-start.11 = (bf16[2,225,512]{2,1,0:T(8,128)(2,1)S(1)}, bf16[2,225,512]{2,1,0:T(8,128)(2,1)S(1)}, u32[]{:S(2)}, u32[]{:S(2)}) collective-permute-start(bf16[2,225,512]{2,1,0:T(8,128)(2,1)S(1)} %collective-permute-done.9.refs_4_), channel_id=1, source_target_pairs={{0,224},{32,0},{64,32},{96,64},{128,96},{160,128},{192,160},{224,1... | collective-permute-start | bytes 1382408 | tf_op jit(solution)/shard_map/ppermute | solution.py:21
  66.6 20.0 %collective-permute-done.16 = bf16[64,1800]{1,0:T(8,128)(2,1)S(1)} collective-permute-done((bf16[64,1800]{1,0:T(8,128)(2,1)S(1)}, bf16[64,1800]{1,0:T(8,128)(2,1)S(1)}, u32[]{:S(2)}, u32[]{:S(2)}) %collective-permute-start.16) | collective-permute-done | bytes 230432 | tf_op jit(solution)/shard_map/ppermute | solution.py:21
  86.9 3.6 %collective-permute-start.21 = (bf16[32,1800]{1,0:T(8,128)(2,1)S(1)}, bf16[32,1800]{1,0:T(8,128)(2,1)S(1)}, u32[]{:S(2)}, u32[]{:S(2)}) collective-permute-start(bf16[32,1800]{1,0:T(8,128)(2,1)S(1)} %slice.26), channel_id=1, source_target_pairs={{0,224},{32,0},{64,32},{96,64},{128,96},{160,128},{192,160},{224,1... | collective-permute-start | bytes 345608 | tf_op jit(solution)/shard_map/ppermute | solution.py:21
  90.5 3.2 %collective-permute-start.6 = (bf16[2,225,512]{2,1,0:T(8,128)(2,1)S(1)}, bf16[2,225,512]{2,1,0:T(8,128)(2,1)}, u32[]{:S(2)}, u32[]{:S(2)}) collective-permute-start(bf16[2,225,512]{2,1,0:T(8,128)(2,1)S(1)} %collective-permute-done.5.refs_9_), channel_id=1, source_target_pairs={{0,224},{32,0},{64,32},{96,64},{128,96},{160,128},{192,160},{224,1... | collective-permute-start | bytes 1382408 | tf_op jit(solution)/shard_map/ppermute | solution.py:21
  93.9 3.1 %collective-permute-start.13 = (bf16[2,225,512]{2,1,0:T(8,128)(2,1)S(1)}, bf16[2,225,512]{2,1,0:T(8,128)(2,1)S(1)}, u32[]{:S(2)}, u32[]{:S(2)}) collective-permute-start(bf16[2,225,512]{2,1,0:T(8,128)(2,1)S(1)} %collective-permute-done.11.refs_8_), channel_id=1, source_target_pairs={{0,224},{32,0},{64,32},{96,64},{128,96},{160,128},{192,160},{224,1... | collective-permute-start | bytes 1382408 | tf_op jit(solution)/shard_map/ppermute | solution.py:21
  97.0 1.0 constant_dynamic-update-slice_fusion
  98.0 1.3 fusion
  99.3 6.3 %collective-permute-done.2.refs_10_ = bf16[2,225,512]{2,1,0:T(8,128)(2,1)} collective-permute-done((bf16[2,225,512]{2,1,0:T(8,128)(2,1)S(1)}, bf16[2,225,512]{2,1,0:T(8,128)(2,1)}, u32[]{:S(2)}, u32[]{:S(2)}) %collective-permute-start.2) | collective-permute-done | bytes 460832 | tf_op jit(solution)/shard_map/ppermute | solution.py:21
  105.6 3.2 %collective-permute-start.7 = (bf16[2,225,512]{2,1,0:T(8,128)(2,1)}, bf16[2,225,512]{2,1,0:T(8,128)(2,1)}, u32[]{:S(2)}, u32[]{:S(2)}) collective-permute-start(bf16[2,225,512]{2,1,0:T(8,128)(2,1)} %collective-permute-done.6.refs_13_), channel_id=1, source_target_pairs={{0,224},{32,0},{64,32},{96,64},{128,96},{160,128},{192,160},{224,1... | collective-permute-start | bytes 1382408 | tf_op jit(solution)/shard_map/ppermute | solution.py:21
  108.8 6.8 %collective-permute-done.12.refs_11_ = bf16[2,225,512]{2,1,0:T(8,128)(2,1)S(1)} collective-permute-done((bf16[2,225,512]{2,1,0:T(8,128)(2,1)S(1)}, bf16[2,225,512]{2,1,0:T(8,128)(2,1)S(1)}, u32[]{:S(2)}, u32[]{:S(2)}) %collective-permute-start.12) | collective-permute-done | bytes 460832 | tf_op jit(solution)/shard_map/ppermute | solution.py:21
  115.6 0.8 copy-done.6
  116.4 0.8 copy-done.8
  117.2 1.0 copy-done.1
  118.2 1.0 copy-done.3
  119.3 1.0 copy-done.5
  120.3 1.0 copy-done.7
  121.3 1.0 copy-done.9
  122.3 12.4 %shard_map.68.refs_2_ = f32[800,512]{1,0:T(8,128)S(1)} custom-call(s32[7]{0:T(128)S(1)} %stack.35.owner_ref, bf16[32,800,225]{2,1,0:T(8,128)(2,1)} %bitcast.17, bf16[2,225,512]{2,1,0:T(8,128)(2,1)S(1)} %reshape.62.refs_0_, bf16[2,225,512]{2,1,0:T(8,128)(2,1)S(1)} %reshape.63.refs_1_, bf16[2,225,512]{2,1,0:T(8,128)(2,1)S(1)} %collective-permute-done.refs_2_, ...), custom_call_target="tpu_custom_call" | custom-call | flops 5160960000 | bytes 16531200 | tf_op jit(solution)/shard_map/pallas_call | solution.py:79
  134.7 4.7 %shard_map.69 = bf16[800,512]{1,0:T(8,128)(2,1)} custom-call(s32[1]{0:T(128)} %bitcast.owner_ref, bf16[32,800,225]{2,1,0:T(8,128)(2,1)} %bitcast.18, bf16[2,225,512]{2,1,0:T(8,128)(2,1)} %collective-permute-done.3.refs_0_, bf16[2,225,512]{2,1,0:T(8,128)(2,1)} %collective-permute-done.7.refs_1_, f32[800,512]{1,0:T(8,128)S(1)} %shard_map.68.refs_2_), custom_call_target="tpu_custom_call" | custom-call | flops 737280000 | bytes 2361600 | tf_op jit(solution)/shard_map/pallas_call | solution.py:79
  (78 shorter events, 3.7 us)
Async XLA Ops:
  7.2 110.0 %all-gather.2.cloned.1.call-start = ((), (), s32[]{:S(2)}) async-start(), calls=%async_computation.1 | async-start | bytes 13516800 | tf_op jit(solution)/shard_map/all_gather | solution.py:101
  7.9 7.6 %copy-start.10 = (bf16[800,225]{1,0:T(8,128)(2,1)S(1)}, bf16[800,225]{1,0:T(8,128)(2,1)}, u32[]{:S(2)}) copy-start(bf16[800,225]{1,0:T(8,128)(2,1)} %param.5) | copy-start | bytes 1080004
  9.2 14.9 %copy-start.13 = (s32[100]{0:T(128)S(1)}, s32[100]{0:T(128)}, u32[]{:S(2)}) copy-start(s32[100]{0:T(128)} %param.8) | copy-start | bytes 1204
  9.2 15.0 %slice-start = ((s32[900]{0:T(1024)}), s32[8]{0:T(128)S(1)}, s32[]{:S(2)}) async-start(s32[900]{0:T(1024)} %param.9), calls=%async_computation.2 | async-start | bytes 1024 | tf_op jit(solution)/shard_map/slice | solution.py:152
  9.4 46.0 %collective-permute-start.4 = (bf16[2,225,512]{2,1,0:T(8,128)(2,1)S(1)}, bf16[2,225,512]{2,1,0:T(8,128)(2,1)S(1)}, u32[]{:S(2)}, u32[]{:S(2)}) collective-permute-start(bf16[2,225,512]{2,1,0:T(8,128)(2,1)S(1)} %reshape.63.refs_1_), channel_id=1, source_target_pairs={{0,224},{32,0},{64,32},{96,64},{128,96},{160,128},{192,160},{224,1... | collective-permute-start | bytes 1382408 | tf_op jit(solution)/shard_map/ppermute | solution.py:21
  15.3 40.2 %collective-permute-start.8 = (bf16[2,225,512]{2,1,0:T(8,128)(2,1)S(1)}, bf16[2,225,512]{2,1,0:T(8,128)(2,1)S(1)}, u32[]{:S(2)}, u32[]{:S(2)}) collective-permute-start(bf16[2,225,512]{2,1,0:T(8,128)(2,1)S(1)} %reshape.63.refs_1_), channel_id=1, source_target_pairs={{0,32},{32,64},{64,96},{96,128},{128,160},{160,192},{192,224},{224... | collective-permute-start | bytes 1382408 | tf_op jit(solution)/shard_map/ppermute | solution.py:21
  15.4 30.6 %collective-permute-start = (bf16[2,225,512]{2,1,0:T(8,128)(2,1)S(1)}, bf16[2,225,512]{2,1,0:T(8,128)(2,1)S(1)}, u32[]{:S(2)}, u32[]{:S(2)}) collective-permute-start(bf16[2,225,512]{2,1,0:T(8,128)(2,1)S(1)} %reshape.62.refs_0_), channel_id=1, source_target_pairs={{0,32},{32,64},{64,96},{96,128},{128,160},{160,192},{192,224},{224... | collective-permute-start | bytes 1382408 | tf_op jit(solution)/shard_map/ppermute | solution.py:21
  15.6 21.0 %copy-start.12 = (s32[900]{0:T(1024)S(1)}, s32[900]{0:T(1024)}, u32[]{:S(2)}) copy-start(s32[900]{0:T(1024)} %param.9) | copy-start | bytes 10804
  16.5 15.9 %all-to-all-start = ((bf16[8,64,225]{2,0,1:T(8,128)(2,1)}), bf16[8,64,225]{2,0,1:T(8,128)(2,1)S(1)}, u32[]{:S(2)}, u32[]{:S(2)}) async-start(bf16[8,64,225]{2,0,1:T(8,128)(2,1)} %copy.9), calls=%async_computation | async-start | bytes 524288 | tf_op jit(solution)/shard_map/all_to_all | solution.py:109
  33.4 8.7 %collective-permute-start.14 = (bf16[64,1800]{1,0:T(8,128)(2,1)S(1)}, bf16[64,1800]{1,0:T(8,128)(2,1)}, u32[]{:S(2)}, u32[]{:S(2)}) collective-permute-start(bf16[64,1800]{1,0:T(8,128)(2,1)S(1)} %reshape.66), channel_id=1, source_target_pairs={{0,224},{32,0},{64,32},{96,64},{128,96},{160,128},{192,160},{224,1... | collective-permute-start | bytes 691208 | tf_op jit(solution)/shard_map/ppermute | solution.py:21
  36.5 9.5 %collective-permute-start.17 = (bf16[64,1800]{1,0:T(8,128)(2,1)S(1)}, bf16[64,1800]{1,0:T(8,128)(2,1)}, u32[]{:S(2)}, u32[]{:S(2)}) collective-permute-start(bf16[64,1800]{1,0:T(8,128)(2,1)S(1)} %reshape.66), channel_id=1, source_target_pairs={{0,32},{32,64},{64,96},{96,128},{128,160},{160,192},{192,224},{224... | collective-permute-start | bytes 691208 | tf_op jit(solution)/shard_map/ppermute | solution.py:21
  42.2 16.7 %collective-permute-start.9 = (bf16[2,225,512]{2,1,0:T(8,128)(2,1)S(1)}, bf16[2,225,512]{2,1,0:T(8,128)(2,1)S(1)}, u32[]{:S(2)}, u32[]{:S(2)}) collective-permute-start(bf16[2,225,512]{2,1,0:T(8,128)(2,1)S(1)} %reshape.62.refs_0_), channel_id=1, source_target_pairs={{0,224},{32,0},{64,32},{96,64},{128,96},{160,128},{192,160},{224,1... | collective-permute-start | bytes 1382408 | tf_op jit(solution)/shard_map/ppermute | solution.py:21
  46.0 8.5 %collective-permute-start.18 = (bf16[64,1800]{1,0:T(8,128)(2,1)}, bf16[64,1800]{1,0:T(8,128)(2,1)S(1)}, u32[]{:S(2)}, u32[]{:S(2)}) collective-permute-start(bf16[64,1800]{1,0:T(8,128)(2,1)} %collective-permute-done.17), channel_id=1, source_target_pairs={{0,32},{32,64},{64,96},{96,128},{128,160},{160,192},{192,224},{224... | collective-permute-start | bytes 691208 | tf_op jit(solution)/shard_map/ppermute | solution.py:21
  46.0 52.0 %copy-start.11 = (bf16[64,512]{1,0:T(8,128)(2,1)S(1)}, bf16[64,512]{1,0:T(8,128)(2,1)}, u32[]{:S(2)}) copy-start(bf16[64,512]{1,0:T(8,128)(2,1)} %param.7) | copy-start | bytes 196612
  46.0 16.6 %collective-permute-start.15 = (bf16[64,1800]{1,0:T(8,128)(2,1)}, bf16[64,1800]{1,0:T(8,128)(2,1)S(1)}, u32[]{:S(2)}, u32[]{:S(2)}) collective-permute-start(bf16[64,1800]{1,0:T(8,128)(2,1)} %collective-permute-done.14), channel_id=1, source_target_pairs={{0,224},{32,0},{64,32},{96,64},{128,96},{160,128},{192,160},{224,1... | collective-permute-start | bytes 691208 | tf_op jit(solution)/shard_map/ppermute | solution.py:21
  54.4 11.8 %collective-permute-start.19 = (bf16[64,1800]{1,0:T(8,128)(2,1)S(1)}, bf16[64,1800]{1,0:T(8,128)(2,1)S(1)}, u32[]{:S(2)}, u32[]{:S(2)}) collective-permute-start(bf16[64,1800]{1,0:T(8,128)(2,1)S(1)} %collective-permute-done.18), channel_id=1, source_target_pairs={{0,32},{32,64},{64,96},{96,128},{128,160},{160,192},{192,224},{224... | collective-permute-start | bytes 691208 | tf_op jit(solution)/shard_map/ppermute | solution.py:21
  55.4 31.5 %collective-permute-start.1 = (bf16[2,225,512]{2,1,0:T(8,128)(2,1)S(1)}, bf16[2,225,512]{2,1,0:T(8,128)(2,1)S(1)}, u32[]{:S(2)}, u32[]{:S(2)}) collective-permute-start(bf16[2,225,512]{2,1,0:T(8,128)(2,1)S(1)} %collective-permute-done.refs_2_), channel_id=1, source_target_pairs={{0,32},{32,64},{64,96},{96,128},{128,160},{160,192},{192,224},{224... | collective-permute-start | bytes 1382408 | tf_op jit(solution)/shard_map/ppermute | solution.py:21
  55.5 34.9 %collective-permute-start.5 = (bf16[2,225,512]{2,1,0:T(8,128)(2,1)S(1)}, bf16[2,225,512]{2,1,0:T(8,128)(2,1)S(1)}, u32[]{:S(2)}, u32[]{:S(2)}) collective-permute-start(bf16[2,225,512]{2,1,0:T(8,128)(2,1)S(1)} %collective-permute-done.4.refs_5_), channel_id=1, source_target_pairs={{0,224},{32,0},{64,32},{96,64},{128,96},{160,128},{192,160},{224,1... | collective-permute-start | bytes 1382408 | tf_op jit(solution)/shard_map/ppermute | solution.py:21
  58.8 31.6 %collective-permute-start.10 = (bf16[2,225,512]{2,1,0:T(8,128)(2,1)S(1)}, bf16[2,225,512]{2,1,0:T(8,128)(2,1)S(1)}, u32[]{:S(2)}, u32[]{:S(2)}) collective-permute-start(bf16[2,225,512]{2,1,0:T(8,128)(2,1)S(1)} %collective-permute-done.8.refs_3_), channel_id=1, source_target_pairs={{0,32},{32,64},{64,96},{96,128},{128,160},{160,192},{192,224},{224... | collective-permute-start | bytes 1382408 | tf_op jit(solution)/shard_map/ppermute | solution.py:21
  62.6 31.0 %collective-permute-start.11 = (bf16[2,225,512]{2,1,0:T(8,128)(2,1)S(1)}, bf16[2,225,512]{2,1,0:T(8,128)(2,1)S(1)}, u32[]{:S(2)}, u32[]{:S(2)}) collective-permute-start(bf16[2,225,512]{2,1,0:T(8,128)(2,1)S(1)} %collective-permute-done.9.refs_4_), channel_id=1, source_target_pairs={{0,224},{32,0},{64,32},{96,64},{128,96},{160,128},{192,160},{224,1... | collective-permute-start | bytes 1382408 | tf_op jit(solution)/shard_map/ppermute | solution.py:21
  66.2 20.4 %collective-permute-start.16 = (bf16[64,1800]{1,0:T(8,128)(2,1)S(1)}, bf16[64,1800]{1,0:T(8,128)(2,1)S(1)}, u32[]{:S(2)}, u32[]{:S(2)}) collective-permute-start(bf16[64,1800]{1,0:T(8,128)(2,1)S(1)} %collective-permute-done.15), channel_id=1, source_target_pairs={{0,224},{32,0},{64,32},{96,64},{128,96},{160,128},{192,160},{224,1... | collective-permute-start | bytes 691208 | tf_op jit(solution)/shard_map/ppermute | solution.py:21
  86.6 7.2 %collective-permute-start.20 = (bf16[32,1800]{1,0:T(8,128)(2,1)S(1)}, bf16[32,1800]{1,0:T(8,128)(2,1)S(1)}, u32[]{:S(2)}, u32[]{:S(2)}) collective-permute-start(bf16[32,1800]{1,0:T(8,128)(2,1)S(1)} %slice.25), channel_id=1, source_target_pairs={{0,32},{32,64},{64,96},{96,128},{128,160},{160,192},{192,224},{224... | collective-permute-start | bytes 345608 | tf_op jit(solution)/shard_map/ppermute | solution.py:21
  86.9 10.1 %collective-permute-start.21 = (bf16[32,1800]{1,0:T(8,128)(2,1)S(1)}, bf16[32,1800]{1,0:T(8,128)(2,1)S(1)}, u32[]{:S(2)}, u32[]{:S(2)}) collective-permute-start(bf16[32,1800]{1,0:T(8,128)(2,1)S(1)} %slice.26), channel_id=1, source_target_pairs={{0,224},{32,0},{64,32},{96,64},{128,96},{160,128},{192,160},{224,1... | collective-permute-start | bytes 345608 | tf_op jit(solution)/shard_map/ppermute | solution.py:21
  90.4 8.8 %copy-start = (bf16[2,225,512]{2,1,0:T(8,128)(2,1)}, bf16[2,225,512]{2,1,0:T(8,128)(2,1)S(1)}, u32[]{:S(2)}) copy-start(bf16[2,225,512]{2,1,0:T(8,128)(2,1)S(1)} %collective-permute-done.5.refs_9_) | copy-start | bytes 1382404
  90.4 15.1 %collective-permute-start.2 = (bf16[2,225,512]{2,1,0:T(8,128)(2,1)S(1)}, bf16[2,225,512]{2,1,0:T(8,128)(2,1)}, u32[]{:S(2)}, u32[]{:S(2)}) collective-permute-start(bf16[2,225,512]{2,1,0:T(8,128)(2,1)S(1)} %collective-permute-done.1.refs_6_), channel_id=1, source_target_pairs={{0,32},{32,64},{64,96},{96,128},{128,160},{160,192},{192,224},{224... | collective-permute-start | bytes 1382408 | tf_op jit(solution)/shard_map/ppermute | solution.py:21
  90.5 8.8 %copy-start.2 = (bf16[2,225,512]{2,1,0:T(8,128)(2,1)}, bf16[2,225,512]{2,1,0:T(8,128)(2,1)S(1)}, u32[]{:S(2)}) copy-start(bf16[2,225,512]{2,1,0:T(8,128)(2,1)S(1)} %collective-permute-done.10.refs_7_) | copy-start | bytes 1382404
  90.5 15.1 %collective-permute-start.6 = (bf16[2,225,512]{2,1,0:T(8,128)(2,1)S(1)}, bf16[2,225,512]{2,1,0:T(8,128)(2,1)}, u32[]{:S(2)}, u32[]{:S(2)}) collective-permute-start(bf16[2,225,512]{2,1,0:T(8,128)(2,1)S(1)} %collective-permute-done.5.refs_9_), channel_id=1, source_target_pairs={{0,224},{32,0},{64,32},{96,64},{128,96},{160,128},{192,160},{224,1... | collective-permute-start | bytes 1382408 | tf_op jit(solution)/shard_map/ppermute | solution.py:21
  93.7 5.6 %copy-start.4 = (bf16[2,225,512]{2,1,0:T(8,128)(2,1)}, bf16[2,225,512]{2,1,0:T(8,128)(2,1)S(1)}, u32[]{:S(2)}) copy-start(bf16[2,225,512]{2,1,0:T(8,128)(2,1)S(1)} %collective-permute-done.11.refs_8_) | copy-start | bytes 1382404
  93.7 21.9 %collective-permute-start.12 = (bf16[2,225,512]{2,1,0:T(8,128)(2,1)S(1)}, bf16[2,225,512]{2,1,0:T(8,128)(2,1)S(1)}, u32[]{:S(2)}, u32[]{:S(2)}) collective-permute-start(bf16[2,225,512]{2,1,0:T(8,128)(2,1)S(1)} %collective-permute-done.10.refs_7_), channel_id=1, source_target_pairs={{0,32},{32,64},{64,96},{96,128},{128,160},{160,192},{192,224},{224... | collective-permute-start | bytes 1382408 | tf_op jit(solution)/shard_map/ppermute | solution.py:21
  93.9 22.6 %collective-permute-start.13 = (bf16[2,225,512]{2,1,0:T(8,128)(2,1)S(1)}, bf16[2,225,512]{2,1,0:T(8,128)(2,1)S(1)}, u32[]{:S(2)}, u32[]{:S(2)}) collective-permute-start(bf16[2,225,512]{2,1,0:T(8,128)(2,1)S(1)} %collective-permute-done.11.refs_8_), channel_id=1, source_target_pairs={{0,224},{32,0},{64,32},{96,64},{128,96},{160,128},{192,160},{224,1... | collective-permute-start | bytes 1382408 | tf_op jit(solution)/shard_map/ppermute | solution.py:21
  105.6 29.1 %collective-permute-start.3 = (bf16[2,225,512]{2,1,0:T(8,128)(2,1)}, bf16[2,225,512]{2,1,0:T(8,128)(2,1)}, u32[]{:S(2)}, u32[]{:S(2)}) collective-permute-start(bf16[2,225,512]{2,1,0:T(8,128)(2,1)} %collective-permute-done.2.refs_10_), channel_id=1, source_target_pairs={{0,32},{32,64},{64,96},{96,128},{128,160},{160,192},{192,224},{224... | collective-permute-start | bytes 1382408 | tf_op jit(solution)/shard_map/ppermute | solution.py:21
  105.6 29.1 %collective-permute-start.7 = (bf16[2,225,512]{2,1,0:T(8,128)(2,1)}, bf16[2,225,512]{2,1,0:T(8,128)(2,1)}, u32[]{:S(2)}, u32[]{:S(2)}) collective-permute-start(bf16[2,225,512]{2,1,0:T(8,128)(2,1)} %collective-permute-done.6.refs_13_), channel_id=1, source_target_pairs={{0,224},{32,0},{64,32},{96,64},{128,96},{160,128},{192,160},{224,1... | collective-permute-start | bytes 1382408 | tf_op jit(solution)/shard_map/ppermute | solution.py:21
  (7 other events, 6.7 us)
Sparse Core Ops, SparseCore 0:
  10.6 71.9 all-gather.1

commit v2 on v1

v2 whole, which is shorter than its diff:
```python
import functools

import jax
import jax.numpy as jnp
from jax import lax
from jax.experimental import pallas as pl
from jax.experimental.pallas import tpu as pltpu
from jax.sharding import PartitionSpec as P

NO = 100
NV = 900
JW = 64
CW = 8
RING = 8
QUARTERS = 4
LANES = 256
OFFSETS = (0, -1, 1, -2, 2, -3, 3, 4, 4)
UP = [(i, (i + 1) % RING) for i in range(RING)]
DOWN = [(i, (i - 1) % RING) for i in range(RING)]
WHOLE = pl.BlockSpec(memory_space=pltpu.VMEM)


def shift(value, step):
    return lax.ppermute(value, "row", UP if step > 0 else DOWN)


def tie(value, done):
    at = (0,) * value.ndim
    size = (1,) * (value.ndim - 2) + (8, 128)
    corner = lax.slice(value, at, size)
    for other in done:
        first = lax.slice(other, (0,) * other.ndim, (1,) * (other.ndim - 2) + (8, 128))
        corner = corner + first.reshape(size) * jnp.zeros((), value.dtype)
    return lax.dynamic_update_slice(value, corner, at)


def ladder_kernel(n, first, last, owner_ref, amps_ref, *refs):
    blocks, refs = refs[: 2 * n], refs[2 * n :]
    before_ref = None
    if not first:
        before_ref, refs = refs[0], refs[1:]
    out_ref, held, halves, right, sems = refs[:5]
    total = refs[5] if last and n > 1 else out_ref

    def fetch(k):
        start = pl.multiple_of(owner_ref[k] * QUARTERS, QUARTERS)
        copies = [
            pltpu.make_async_copy(
                amps_ref.at[start + q],
                held.at[k % 2, :, pl.ds(LANES * q, LANES)],
                sems.at[k % 2, q],
            )
            for q in range(QUARTERS)
        ]
        copies += [
            pltpu.make_async_copy(blocks[2 * k + h], halves.at[k % 2, h], sems.at[k % 2, QUARTERS + h])
            for h in range(2)
        ]
        return copies

    for c in fetch(0):
        c.start()
    for k in range(n):
        if k + 1 < n:
            for c in fetch(k + 1):
                c.start()
        for c in fetch(k):
            c.wait()
        for q in range(QUARTERS):
            block = halves[k % 2, q // 2, q % 2]
            rest = jnp.zeros((LANES - block.shape[0], block.shape[1]), block.dtype)
            right[LANES * q : LANES * (q + 1), :] = jnp.concatenate([block, rest], axis=0)
        value = jnp.dot(held[k % 2], right[...], preferred_element_type=jnp.float32)
        if k > 0:
            value = value + total[...]
        elif before_ref is not None:
            value = value + before_ref[...]
        if last and k == n - 1:
            out_ref[...] = value.astype(out_ref.dtype)
        else:
            total[...] = value


def ladder_part(owners, amps, blocks, before, last):
    n = len(blocks) // 2
    rows, columns = amps.shape[1], blocks[0].shape[2]
    first = before is None
    depth = QUARTERS * LANES
    scratch = [
        pltpu.VMEM((2, rows, depth), jnp.bfloat16),
        pltpu.VMEM((2, 2) + blocks[0].shape, jnp.bfloat16),
        pltpu.VMEM((depth, columns), jnp.bfloat16),
        pltpu.SemaphoreType.DMA((2, QUARTERS + 2)),
    ]
    if last and n > 1:
        scratch.append(pltpu.VMEM((rows, columns), jnp.float32))
    return pl.pallas_call(
        functools.partial(ladder_kernel, n, first, last),
        out_shape=jax.ShapeDtypeStruct((rows, columns), jnp.bfloat16 if last else jnp.float32),
        in_specs=[pl.BlockSpec(memory_space=pltpu.SMEM), pl.BlockSpec(memory_space=pl.ANY)]
        + [pl.BlockSpec(memory_space=pl.ANY)] * (2 * n)
        + [WHOLE] * (0 if first else 1),
        out_specs=WHOLE,
        scratch_shapes=scratch,
        compiler_params=pltpu.CompilerParams(vmem_limit_bytes=44 << 20),
        cost_estimate=pl.CostEstimate(
            flops=2 * rows * depth * columns * n,
            bytes_accessed=2 * n * depth * (rows + columns),
            transcendentals=0,
        ),
    )(owners, amps, *blocks, *([] if first else [before]))


def cycle_kernel(n, at_ref, occ_ref, low_ref, left_ref, vir_ref, *refs):
    parts, out_ref, right, sems = refs[:n], refs[n], refs[n + 1], refs[n + 2]
    rows = left_ref.shape[0]
    each = right.shape[0] // RING

    def copy(i):
        owner = (at_ref[0] + OFFSETS[i]) & (RING - 1)
        size = parts[i].shape[0]
        start = owner * each + (each // 2 if i == n - 1 else 0)
        return pltpu.make_async_copy(
            parts[i], right.at[pl.ds(pl.multiple_of(start, each // 2), size)], sems.at[i]
        )

    for i in range(n):
        copy(i).start()
    row = lax.broadcasted_iota(jnp.int32, (rows, 128), 0)
    row_label = jnp.zeros((rows, 128), jnp.int32)
    for i in range(rows // CW):
        label = occ_ref[at_ref[0] * (rows // CW) + i]
        for e in range(CW):
            row_label = jnp.where(row == i * CW + e, label ^ low_ref[e], row_label)
    count = out_ref.shape[1] // NV
    labels = [vir_ref[...] ^ occ_ref[at_ref[1] * count + j] for j in range(count)]
    col_label = jnp.concatenate(labels, axis=1)
    allowed = ((row_label[:, :1] ^ col_label) & 7) == 0
    for i in range(n):
        copy(i).wait()
    total = jnp.dot(left_ref[...], right[...], preferred_element_type=jnp.float32)
    out_ref[...] = jnp.where(allowed, total, 0.0).astype(out_ref.dtype)


def cycle_part(at, occ, vir, left, parts):
    rows, columns, depth = left.shape[0], parts[0].shape[1], left.shape[1]
    scalars = pl.BlockSpec(memory_space=pltpu.SMEM)
    return pl.pallas_call(
        functools.partial(cycle_kernel, len(parts)),
        out_shape=jax.ShapeDtypeStruct((rows, columns), jnp.bfloat16),
        in_specs=[scalars] * 3
        + [WHOLE] * 2
        + [pl.BlockSpec(memory_space=pl.ANY)] * len(parts),
        out_specs=WHOLE,
        scratch_shapes=[
            pltpu.VMEM((depth, columns), jnp.bfloat16),
            pltpu.SemaphoreType.DMA((len(parts),)),
        ],
        compiler_params=pltpu.CompilerParams(vmem_limit_bytes=16 << 20),
        cost_estimate=pl.CostEstimate(
            flops=2 * rows * depth * columns,
            bytes_accessed=2 * columns * (depth + rows),
            transcendentals=0,
        ),
    )(at, occ, vir[:CW], left, vir.reshape(1, -1), *parts)


def shards(amplitudes, integrals, cycle_integrals, occ_irrep, vir_irrep):
    rows_here, local_cols = amplitudes.shape
    occ_block = rows_here // NO
    z = lax.axis_index("row")
    p = lax.axis_index(("col", "depth"))

    padded = jnp.pad(amplitudes, ((0, 0), (0, LANES - local_cols)))
    gathered = lax.all_gather(padded, ("col", "depth"), axis=0, tiled=True)
    gathered = gathered.reshape(RING * QUARTERS, rows_here, LANES)

    half = NV // 2
    top = integrals[:half].reshape(2, half // 2, -1)
    bot = integrals[half:].reshape(2, half // 2, -1)

    tops, bots, regrouped = {0: top}, {0: bot}, {}
    for s in range(1, 5):
        tops[-s], bots[s] = shift(tops[1 - s], 1), shift(bots[s - 1], -1)
        if s < 4:
            bots[-s], tops[s] = shift(bots[1 - s], 1), shift(tops[s - 1], -1)
    tops[4] = tops.pop(-4)

    window = amplitudes.reshape(occ_block, NO, local_cols)[:, :JW, :]
    window = tie(window, [tops[-1], bots[1]])
    spread = lax.all_to_all(window, ("col", "depth"), split_axis=1, concat_axis=2, tiled=True)
    occ_here = spread.shape[1]
    columns = occ_here * NV
    ordered = (
        spread.reshape(occ_block, occ_here, CW, NV)
        .transpose(0, 2, 1, 3)
        .reshape(occ_block * CW, columns)
    )
    width = ordered.shape[0] // 2
    regrouped[0] = ordered
    regrouped[-1], regrouped[1] = shift(ordered, 1), shift(ordered, -1)
    regrouped[-1], regrouped[1] = (tie(regrouped[d], [bots[-2], tops[2]]) for d in (-1, 1))
    regrouped[-2], regrouped[2] = shift(regrouped[-1], 1), shift(regrouped[1], -1)
    regrouped[-2], regrouped[2] = (tie(regrouped[d], [tops[-3], bots[3]]) for d in (-2, 2))
    regrouped[-3], regrouped[3] = shift(regrouped[-2], 1), shift(regrouped[2], -1)
    def blocks(offsets):
        return [b for d in offsets for b in (tops[d], bots[d])]

    def owners(offsets):
        return (z + jnp.array(offsets, jnp.int32)) & (RING - 1)

    near, middle, late = [0, -1, 1, -2, 2], [-3, 3], [4]
    total = ladder_part(owners(near), gathered, blocks(near), None, False)
    regrouped[-3], regrouped[3] = (
        tie(regrouped[d], [total[:8, :128].astype(jnp.bfloat16)]) for d in (-3, 3)
    )
    regrouped[4] = [shift(regrouped[-3][:width], 1), shift(regrouped[3][width:], -1)]
    total = ladder_part(owners(middle), gathered, blocks(middle), total, False)
    ladder = ladder_part(owners(late), gathered, blocks(late), total, True)

    parts = [regrouped[d] for d in OFFSETS[:7]] + regrouped[4]
    here = jnp.stack([z, p]).astype(jnp.int32)
    cycle = cycle_part(here, occ_irrep, vir_irrep, cycle_integrals, parts)
    return ladder, cycle


def solution(mesh):
    in_specs = (P("row", ("col", "depth")), P("row", ("col", "depth")), P("row", None), P(), P())
    out_specs = (P("row", ("col", "depth")), P("row", ("col", "depth")))
    return jax.shard_map(shards, mesh=mesh, in_specs=in_specs, out_specs=out_specs, check_vma=False)
```

time: 147 us -> 130 us (0.88)
  waiting for transfers between devices: 56.3 us -> 42.5 us
  local copies, waits for them, and re-layouts: 12.7 us -> 6.04 us
  other arithmetic: 0.15 us -> 2.71 us
  Pallas kernels: 17 us -> 19.4 us
    ppermute x22, waiting for transfers between devices: 47.5 us -> 37.7 us  [shift(): return lax.ppermute(value, 'row', UP if step > 0 else DOWN)]
    unnamed x36 -> x22, local copies, waits for them, and re-layouts: 7.83 us -> 1.86 us
    pallas_call x0 -> x1, Pallas kernels: none -> 3.64 us  [cycle_part(): pl.pallas_call(functools.partial(cycle_kernel, len(parts)), out_shape=jax...]
    all_to_all x1, waiting for transfers between devices: 8.1 us -> 4.8 us  [shards(): lax.all_to_all(window, ('col', 'depth'), split_axis=1, concat_axis=2, til...]
    dynamic_update_slice x0 -> x4, other arithmetic: none -> 2.63 us  [tie(): return lax.dynamic_update_slice(value, corner, at)]
    pad x0 -> x1, local copies, waits for them, and re-layouts: none -> 1.89 us  [shards(): padded = jnp.pad(amplitudes, ((0, 0), (0, LANES - local_cols)))]
    pallas_call x2 -> x3, Pallas kernels: 17 us -> 15.7 us  [ladder_part(): pl.pallas_call(functools.partial(ladder_kernel, n, first, last), out_shap...]
  transfers between devices with their start and end apart: 24 -> 24, of which waited for: 8 -> 9; matrix products, arithmetic and copies ran while one was open for 5% -> 4% of each run, Pallas kernels for 8% -> 12%
where the time goes in v2:
time: 130 us
  starting transfers between devices  44.7 us (34%)
  waiting for transfers between devices  42.5 us (33%)
  Pallas kernels  19.4 us (15%)
  between operations  14.3 us (11%)
  local copies, waits for them, and re-layouts  6.04 us (5%)
  other arithmetic  2.71 us (2%)
    ppermute x22, waiting for transfers between devices, shift(): return lax.ppermute(value, 'row', UP if step > 0 else DOWN)  37.7 us
    ppermute x22, starting transfers between devices, shift(): return lax.ppermute(value, 'row', UP if step > 0 else DOWN)  37 us
    pallas_call x3, Pallas kernels, ladder_part(): pl.pallas_call(functools.partial(ladder_kernel, n, first, last), out_shap...  15.7 us
    all_to_all x1, starting transfers between devices, shards(): lax.all_to_all(window, ('col', 'depth'), split_axis=1, concat_axis=2, til...  7.62 us
    all_to_all x1, waiting for transfers between devices, shards(): lax.all_to_all(window, ('col', 'depth'), split_axis=1, concat_axis=2, til...  4.8 us
    pallas_call x1, Pallas kernels, cycle_part(): pl.pallas_call(functools.partial(cycle_kernel, len(parts)), out_shape=jax...  3.64 us
    dynamic_update_slice x4, other arithmetic, tie(): return lax.dynamic_update_slice(value, corner, at)  2.63 us
  transfers between devices with their start and end apart: 24, of which 9 were waited for; matrix products, arithmetic and copies ran while one was open for 4% of the time, Pallas kernels for 12%

profile of v2, /device:TPU:2, one launch (start us, length us, event | category | flops | bytes accessed | tf_op | source)
XLA Modules:
  0.0 129.7 jit_solution(10797205251561530382)
XLA Ops:
  7.2 1.9 %pad.4 = bf16[800,256]{1,0:T(8,128)(2,1)} pad(bf16[800,225]{1,0:T(8,128)(2,1)} %param.8, bf16[]{:T(256)} %constant.10.clone.1), padding=0_0x0_31 | pad | bytes 769602 | tf_op jit(solution)/shard_map/jit(_pad)/pad | solution.py:174
  9.4 2.0 %collective-permute-start = (bf16[2,225,512]{2,1,0:T(8,128)(2,1)S(1)}, bf16[2,225,512]{2,1,0:T(8,128)(2,1)S(1)}, u32[]{:S(2)}, u32[]{:S(2)}) collective-permute-start(bf16[2,225,512]{2,1,0:T(8,128)(2,1)S(1)} %reshape.43.refs_0_), channel_id=1, source_target_pairs={{0,32},{32,64},{64,96},{96,128},{128,160},{160,192},{192,224},{224... | collective-permute-start | bytes 1382408 | tf_op jit(solution)/shard_map/ppermute | solution.py:24
  11.5 4.0 %collective-permute-start.4 = (bf16[2,225,512]{2,1,0:T(8,128)(2,1)S(1)}, bf16[2,225,512]{2,1,0:T(8,128)(2,1)S(1)}, u32[]{:S(2)}, u32[]{:S(2)}) collective-permute-start(bf16[2,225,512]{2,1,0:T(8,128)(2,1)S(1)} %reshape.44.refs_1_), channel_id=1, source_target_pairs={{0,224},{32,0},{64,32},{96,64},{128,96},{160,128},{192,160},{224,1... | collective-permute-start | bytes 1382408 | tf_op jit(solution)/shard_map/ppermute | solution.py:24
  15.5 2.0 %collective-permute-start.11 = (bf16[2,225,512]{2,1,0:T(8,128)(2,1)S(1)}, bf16[2,225,512]{2,1,0:T(8,128)(2,1)}, u32[]{:S(2)}, u32[]{:S(2)}) collective-permute-start(bf16[2,225,512]{2,1,0:T(8,128)(2,1)S(1)} %reshape.43.refs_0_), channel_id=1, source_target_pairs={{0,224},{32,0},{64,32},{96,64},{128,96},{160,128},{192,160},{224,1... | collective-permute-start | bytes 1382408 | tf_op jit(solution)/shard_map/ppermute | solution.py:24
  17.7 9.3 %collective-permute-done.refs_2_ = bf16[2,225,512]{2,1,0:T(8,128)(2,1)S(1)} collective-permute-done((bf16[2,225,512]{2,1,0:T(8,128)(2,1)S(1)}, bf16[2,225,512]{2,1,0:T(8,128)(2,1)S(1)}, u32[]{:S(2)}, u32[]{:S(2)}) %collective-permute-start) | collective-permute-done | bytes 460832 | tf_op jit(solution)/shard_map/ppermute | solution.py:24
  27.9 7.6 %all-to-all-start = ((bf16[8,64,225]{2,0,1:T(8,128)(2,1)}), bf16[8,64,225]{2,0,1:T(8,128)(2,1)S(1)}, u32[]{:S(2)}, u32[]{:S(2)}) async-start(bf16[8,64,225]{2,0,1:T(8,128)(2,1)} %copy.12), calls=%async_computation | async-start | bytes 524288 | tf_op jit(solution)/shard_map/all_to_all | solution.py:191
  35.8 3.3 %collective-permute-start.5 = (bf16[2,225,512]{2,1,0:T(8,128)(2,1)S(1)}, bf16[2,225,512]{2,1,0:T(8,128)(2,1)}, u32[]{:S(2)}, u32[]{:S(2)}) collective-permute-start(bf16[2,225,512]{2,1,0:T(8,128)(2,1)S(1)} %collective-permute-done.4.refs_5_), channel_id=1, source_target_pairs={{0,224},{32,0},{64,32},{96,64},{128,96},{160,128},{192,160},{224,1... | collective-permute-start | bytes 1382408 | tf_op jit(solution)/shard_map/ppermute | solution.py:24
  39.1 4.8 %all-to-all-done = bf16[8,64,225]{2,0,1:T(8,128)(2,1)S(1)} async-done(((bf16[8,64,225]{2,0,1:T(8,128)(2,1)}), bf16[8,64,225]{2,0,1:T(8,128)(2,1)S(1)}, u32[]{:S(2)}, u32[]{:S(2)}) %all-to-all-start) | async-done | bytes 230432 | tf_op jit(solution)/shard_map/all_to_all | solution.py:191
  45.0 1.2 collective-permute-start.14
  46.1 2.4 %collective-permute-start.12 = (bf16[2,225,512]{2,1,0:T(8,128)(2,1)}, bf16[2,225,512]{2,1,0:T(8,128)(2,1)S(1)}, u32[]{:S(2)}, u32[]{:S(2)}) collective-permute-start(bf16[2,225,512]{2,1,0:T(8,128)(2,1)} %collective-permute-done.11.refs_4_), channel_id=1, source_target_pairs={{0,224},{32,0},{64,32},{96,64},{128,96},{160,128},{192,160},{224,1... | collective-permute-start | bytes 1382408 | tf_op jit(solution)/shard_map/ppermute | solution.py:24
  48.5 7.5 %collective-permute-done.14 = bf16[64,1800]{1,0:T(8,128)(2,1)S(1)} collective-permute-done((bf16[64,1800]{1,0:T(8,128)(2,1)S(1)}, bf16[64,1800]{1,0:T(8,128)(2,1)S(1)}, u32[]{:S(2)}, u32[]{:S(2)}) %collective-permute-start.14) | collective-permute-done | bytes 230432 | tf_op jit(solution)/shard_map/ppermute | solution.py:24
  56.0 2.1 %collective-permute-start.15 = (bf16[64,1800]{1,0:T(8,128)(2,1)S(1)}, bf16[64,1800]{1,0:T(8,128)(2,1)}, u32[]{:S(2)}, u32[]{:S(2)}) collective-permute-start(bf16[64,1800]{1,0:T(8,128)(2,1)S(1)} %reshape.48.refs_0_), channel_id=1, source_target_pairs={{0,224},{32,0},{64,32},{96,64},{128,96},{160,128},{192,160},{224,1... | collective-permute-start | bytes 691208 | tf_op jit(solution)/shard_map/ppermute | solution.py:24
  58.0 3.2 %collective-permute-start.6 = (bf16[2,225,512]{2,1,0:T(8,128)(2,1)}, bf16[2,225,512]{2,1,0:T(8,128)(2,1)}, u32[]{:S(2)}, u32[]{:S(2)}) collective-permute-start(bf16[2,225,512]{2,1,0:T(8,128)(2,1)} %collective-permute-done.5.refs_9_), channel_id=1, source_target_pairs={{0,224},{32,0},{64,32},{96,64},{128,96},{160,128},{192,160},{224,1... | collective-permute-start | bytes 1382408 | tf_op jit(solution)/shard_map/ppermute | solution.py:24
  61.3 4.5 %collective-permute-done.15 = bf16[64,1800]{1,0:T(8,128)(2,1)} collective-permute-done((bf16[64,1800]{1,0:T(8,128)(2,1)S(1)}, bf16[64,1800]{1,0:T(8,128)(2,1)}, u32[]{:S(2)}, u32[]{:S(2)}) %collective-permute-start.15) | collective-permute-done | bytes 230432 | tf_op jit(solution)/shard_map/ppermute | solution.py:24
  66.9 1.2 fusion.10
  68.2 3.2 %collective-permute-start.16 = (bf16[64,1800]{1,0:T(8,128)(2,1)S(1)}, bf16[64,1800]{1,0:T(8,128)(2,1)}, u32[]{:S(2)}, u32[]{:S(2)}) collective-permute-start(bf16[64,1800]{1,0:T(8,128)(2,1)S(1)} %get-tuple-element.7.refs_1_), channel_id=1, source_target_pairs={{0,32},{32,64},{64,96},{96,128},{128,160},{160,192},{192,224},{224... | collective-permute-start | bytes 691208 | tf_op jit(solution)/shard_map/ppermute | solution.py:24
  71.5 9.7 %collective-permute-done.16 = bf16[64,1800]{1,0:T(8,128)(2,1)} collective-permute-done((bf16[64,1800]{1,0:T(8,128)(2,1)S(1)}, bf16[64,1800]{1,0:T(8,128)(2,1)}, u32[]{:S(2)}, u32[]{:S(2)}) %collective-permute-start.16) | collective-permute-done | bytes 230432 | tf_op jit(solution)/shard_map/ppermute | solution.py:24
  81.3 1.4 %fusion.4 = (bf16[64,1800]{1,0:T(8,128)(2,1)}, bf16[64,1800]{1,0:T(8,128)(2,1)}) fusion(bf16[64,1800]{1,0:T(8,128)(2,1)} %collective-permute-done.17, bf16[2,225,512]{2,1,0:T(8,128)(2,1)S(1)} %collective-permute-done.2.refs_0_, bf16[2,225,512]{2,1,0:T(8,128)(2,1)} %collective-permute-done.6.refs_3_, bf16[64,1800]{1,0:T(8,128)(2,1)} %collective-permute-done.16), kind=kLoop, calls=%fused_computation.9 | loop fusion | flops 17408 | bytes 12288 | tf_op jit(solution)/shard_map/dynamic_update_slice | solution.py:34
  82.6 2.7 %collective-permute-start.18 = (bf16[64,1800]{1,0:T(8,128)(2,1)}, bf16[64,1800]{1,0:T(8,128)(2,1)S(1)}, u32[]{:S(2)}, u32[]{:S(2)}) collective-permute-start(bf16[64,1800]{1,0:T(8,128)(2,1)} %get-tuple-element.5.refs_3_), channel_id=1, source_target_pairs={{0,32},{32,64},{64,96},{96,128},{128,160},{160,192},{192,224},{224... | collective-permute-start | bytes 691208 | tf_op jit(solution)/shard_map/ppermute | solution.py:24
  85.4 1.8 %collective-permute-start.10 = (bf16[2,225,512]{2,1,0:T(8,128)(2,1)}, bf16[2,225,512]{2,1,0:T(8,128)(2,1)}, u32[]{:S(2)}, u32[]{:S(2)}) collective-permute-start(bf16[2,225,512]{2,1,0:T(8,128)(2,1)} %copy-done.2), channel_id=1, source_target_pairs={{0,32},{32,64},{64,96},{96,128},{128,160},{160,192},{192,224},{224... | collective-permute-start | bytes 1382408 | tf_op jit(solution)/shard_map/ppermute | solution.py:24
  87.2 1.5 %collective-permute-start.13 = (bf16[2,225,512]{2,1,0:T(8,128)(2,1)S(1)}, bf16[2,225,512]{2,1,0:T(8,128)(2,1)}, u32[]{:S(2)}, u32[]{:S(2)}) collective-permute-start(bf16[2,225,512]{2,1,0:T(8,128)(2,1)S(1)} %collective-permute-done.12.refs_8_), channel_id=1, source_target_pairs={{0,224},{32,0},{64,32},{96,64},{128,96},{160,128},{192,160},{224,1... | collective-permute-start | bytes 1382408 | tf_op jit(solution)/shard_map/ppermute | solution.py:24
  88.8 2.0 %collective-permute-start.3 = (bf16[2,225,512]{2,1,0:T(8,128)(2,1)}, bf16[2,225,512]{2,1,0:T(8,128)(2,1)}, u32[]{:S(2)}, u32[]{:S(2)}) collective-permute-start(bf16[2,225,512]{2,1,0:T(8,128)(2,1)} %copy-done), channel_id=1, source_target_pairs={{0,32},{32,64},{64,96},{96,128},{128,160},{160,192},{192,224},{224... | collective-permute-start | bytes 1382408 | tf_op jit(solution)/shard_map/ppermute | solution.py:24
  90.8 2.1 %collective-permute-done.18 = bf16[64,1800]{1,0:T(8,128)(2,1)S(1)} collective-permute-done((bf16[64,1800]{1,0:T(8,128)(2,1)}, bf16[64,1800]{1,0:T(8,128)(2,1)S(1)}, u32[]{:S(2)}, u32[]{:S(2)}) %collective-permute-start.18) | collective-permute-done | bytes 230432 | tf_op jit(solution)/shard_map/ppermute | solution.py:24
  92.9 1.8 %collective-permute-start.7 = (bf16[2,225,512]{2,1,0:T(8,128)(2,1)}, bf16[2,225,512]{2,1,0:T(8,128)(2,1)}, u32[]{:S(2)}, u32[]{:S(2)}) collective-permute-start(bf16[2,225,512]{2,1,0:T(8,128)(2,1)} %collective-permute-done.6.refs_3_), channel_id=1, source_target_pairs={{0,224},{32,0},{64,32},{96,64},{128,96},{160,128},{192,160},{224,1... | collective-permute-start | bytes 1382408 | tf_op jit(solution)/shard_map/ppermute | solution.py:24
  95.8 7.8 %shard_map.95.refs_4_ = f32[800,512]{1,0:T(8,128)S(1)} custom-call(s32[5]{0:T(128)S(1)} %add_and_fusion.owner_ref, bf16[32,800,256]{2,1,0:T(8,128)(2,1)} %bitcast.36, bf16[2,225,512]{2,1,0:T(8,128)(2,1)S(1)} %reshape.43.refs_0_, bf16[2,225,512]{2,1,0:T(8,128)(2,1)S(1)} %reshape.44.refs_1_, bf16[2,225,512]{2,1,0:T(8,128)(2,1)S(1)} %collective-permute-done.refs_2_, ...), custom_call_target="tpu_custom_call" | custom-call | flops 4194304000 | bytes 13434880 | tf_op jit(solution)/shard_map/pallas_call | solution.py:97
  103.6 2.7 %collective-permute-done.19 = bf16[64,1800]{1,0:T(8,128)(2,1)S(1)} collective-permute-done((bf16[64,1800]{1,0:T(8,128)(2,1)}, bf16[64,1800]{1,0:T(8,128)(2,1)S(1)}, u32[]{:S(2)}, u32[]{:S(2)}) %collective-permute-start.19) | collective-permute-done | bytes 230432 | tf_op jit(solution)/shard_map/ppermute | solution.py:24
  106.4 1.7 %collective-permute-start.20 = (bf16[32,1800]{1,0:T(8,128)(2,1)S(1)}, bf16[32,1800]{1,0:T(8,128)(2,1)S(1)}, u32[]{:S(2)}, u32[]{:S(2)}) collective-permute-start(bf16[32,1800]{1,0:T(8,128)(2,1)S(1)} %slice.102), channel_id=1, source_target_pairs={{0,32},{32,64},{64,96},{96,128},{128,160},{160,192},{192,224},{224... | collective-permute-start | bytes 345608 | tf_op jit(solution)/shard_map/ppermute | solution.py:24
  108.0 1.7 %collective-permute-start.21 = (bf16[32,1800]{1,0:T(8,128)(2,1)S(1)}, bf16[32,1800]{1,0:T(8,128)(2,1)S(1)}, u32[]{:S(2)}, u32[]{:S(2)}) collective-permute-start(bf16[32,1800]{1,0:T(8,128)(2,1)S(1)} %slice.103), channel_id=1, source_target_pairs={{0,224},{32,0},{64,32},{96,64},{128,96},{160,128},{192,160},{224,1... | collective-permute-start | bytes 345608 | tf_op jit(solution)/shard_map/ppermute | solution.py:24
  109.8 4.3 %shard_map.96.refs_2_ = f32[800,512]{1,0:T(8,128)S(1)} custom-call(s32[2]{0:T(128)S(1)} %add_and_fusion.1.owner_ref, bf16[32,800,256]{2,1,0:T(8,128)(2,1)} %bitcast.37, bf16[2,225,512]{2,1,0:T(8,128)(2,1)S(1)} %copy-done.1, bf16[2,225,512]{2,1,0:T(8,128)(2,1)} %collective-permute-done.10.refs_1_, bf16[2,225,512]{2,1,0:T(8,128)(2,1)} %collective-permute-done.13.refs_2_, ...), custom_call_target="tpu_custom_call" | custom-call | flops 1677721600 | bytes 5373952 | tf_op jit(solution)/shard_map/pallas_call | solution.py:97
  114.1 1.4 %collective-permute-done.7.refs_1_ = bf16[2,225,512]{2,1,0:T(8,128)(2,1)} collective-permute-done((bf16[2,225,512]{2,1,0:T(8,128)(2,1)}, bf16[2,225,512]{2,1,0:T(8,128)(2,1)}, u32[]{:S(2)}, u32[]{:S(2)}) %collective-permute-start.7) | collective-permute-done | bytes 460832 | tf_op jit(solution)/shard_map/ppermute | solution.py:24
  115.4 3.7 %shard_map.97 = bf16[800,512]{1,0:T(8,128)(2,1)} custom-call(s32[1]{0:T(128)S(6)} %and.12.owner_ref, bf16[32,800,256]{2,1,0:T(8,128)(2,1)} %bitcast.38, bf16[2,225,512]{2,1,0:T(8,128)(2,1)} %collective-permute-done.3.refs_0_, bf16[2,225,512]{2,1,0:T(8,128)(2,1)} %collective-permute-done.7.refs_1_, f32[800,512]{1,0:T(8,128)S(1)} %shard_map.96.refs_2_), custom_call_target="tpu_custom_call" | custom-call | flops 838860800 | bytes 2686976 | tf_op jit(solution)/shard_map/pallas_call | solution.py:97
  119.2 3.6 %shard_map.98 = bf16[64,1800]{1,0:T(8,128)(2,1)} custom-call(s32[2]{0:T(128)S(1)} %pad_add_fusion.at_ref, s32[100]{0:T(128)S(1)} %copy-done.6, s32[8]{0:T(128)S(1)} %slice.69.low_ref, bf16[64,512]{1,0:T(8,128)(2,1)S(1)} %copy-done.4, s32[1,900]{1,0:T(1,128)S(1)} %bitcast.35, bf16[64,1800]{1,0:T(8,128)(2,1)S(1)} %reshape.48.refs_0_, ...), custom_call_target="tpu_custom_call" | custom-call | flops 117964800 | bytes 2073600 | tf_op jit(solution)/shard_map/pallas_call | solution.py:148
  (64 shorter events, 5.1 us)
Async XLA Ops:
  7.2 2.0 %copy-start.8 = (bf16[900,512]{1,0:T(8,128)(2,1)S(1)}, bf16[900,512]{1,0:T(8,128)(2,1)}, u32[]{:S(2)}) copy-start(bf16[900,512]{1,0:T(8,128)(2,1)} %param.9) | copy-start | bytes 2764804
  7.2 87.6 %all-gather.2.cloned.1.call-start = ((), (), s32[]{:S(2)}) async-start(), calls=%async_computation.1 | async-start | bytes 13516800 | tf_op jit(solution)/shard_map/all_gather | solution.py:175
  9.1 8.4 %copy-start.7 = (bf16[800,225]{1,0:T(8,128)(2,1)S(1)}, bf16[800,225]{1,0:T(8,128)(2,1)}, u32[]{:S(2)}) copy-start(bf16[800,225]{1,0:T(8,128)(2,1)} %param.8) | copy-start | bytes 1080004
  9.4 17.6 %collective-permute-start = (bf16[2,225,512]{2,1,0:T(8,128)(2,1)S(1)}, bf16[2,225,512]{2,1,0:T(8,128)(2,1)S(1)}, u32[]{:S(2)}, u32[]{:S(2)}) collective-permute-start(bf16[2,225,512]{2,1,0:T(8,128)(2,1)S(1)} %reshape.43.refs_0_), channel_id=1, source_target_pairs={{0,32},{32,64},{64,96},{96,128},{128,160},{160,192},{192,224},{224... | collective-permute-start | bytes 1382408 | tf_op jit(solution)/shard_map/ppermute | solution.py:24
  11.5 15.5 %collective-permute-start.4 = (bf16[2,225,512]{2,1,0:T(8,128)(2,1)S(1)}, bf16[2,225,512]{2,1,0:T(8,128)(2,1)S(1)}, u32[]{:S(2)}, u32[]{:S(2)}) collective-permute-start(bf16[2,225,512]{2,1,0:T(8,128)(2,1)S(1)} %reshape.44.refs_1_), channel_id=1, source_target_pairs={{0,224},{32,0},{64,32},{96,64},{128,96},{160,128},{192,160},{224,1... | collective-permute-start | bytes 1382408 | tf_op jit(solution)/shard_map/ppermute | solution.py:24
  15.5 30.6 %collective-permute-start.11 = (bf16[2,225,512]{2,1,0:T(8,128)(2,1)S(1)}, bf16[2,225,512]{2,1,0:T(8,128)(2,1)}, u32[]{:S(2)}, u32[]{:S(2)}) collective-permute-start(bf16[2,225,512]{2,1,0:T(8,128)(2,1)S(1)} %reshape.43.refs_0_), channel_id=1, source_target_pairs={{0,224},{32,0},{64,32},{96,64},{128,96},{160,128},{192,160},{224,1... | collective-permute-start | bytes 1382408 | tf_op jit(solution)/shard_map/ppermute | solution.py:24
  17.5 31.0 %collective-permute-start.8 = (bf16[2,225,512]{2,1,0:T(8,128)(2,1)S(1)}, bf16[2,225,512]{2,1,0:T(8,128)(2,1)}, u32[]{:S(2)}, u32[]{:S(2)}) collective-permute-start(bf16[2,225,512]{2,1,0:T(8,128)(2,1)S(1)} %reshape.44.refs_1_), channel_id=1, source_target_pairs={{0,32},{32,64},{64,96},{96,128},{128,160},{160,192},{192,224},{224... | collective-permute-start | bytes 1382408 | tf_op jit(solution)/shard_map/ppermute | solution.py:24
  17.7 53.8 %copy-start.10 = (s32[5]{0:T(128)S(1)}, s32[5]{0:T(128)}, u32[]{:S(2)}) copy-start(s32[5]{0:T(128)} %constant.32.clone) | copy-start | bytes 64
  17.7 67.7 %copy-start.5 = (s32[900]{0:T(1024)S(1)}, s32[900]{0:T(1024)}, u32[]{:S(2)}) copy-start(s32[900]{0:T(1024)} %param.12) | copy-start | bytes 10804
  17.7 67.7 %copy-start.9 = (s32[2]{0:T(128)S(1)}, s32[2]{0:T(128)}, u32[]{:S(2)}) copy-start(s32[2]{0:T(128)} %constant.33.clone) | copy-start | bytes 28
  27.9 16.1 %all-to-all-start = ((bf16[8,64,225]{2,0,1:T(8,128)(2,1)}), bf16[8,64,225]{2,0,1:T(8,128)(2,1)S(1)}, u32[]{:S(2)}, u32[]{:S(2)}) async-start(bf16[8,64,225]{2,0,1:T(8,128)(2,1)} %copy.12), calls=%async_computation | async-start | bytes 524288 | tf_op jit(solution)/shard_map/all_to_all | solution.py:191
  35.5 22.5 %collective-permute-start.1 = (bf16[2,225,512]{2,1,0:T(8,128)(2,1)S(1)}, bf16[2,225,512]{2,1,0:T(8,128)(2,1)}, u32[]{:S(2)}, u32[]{:S(2)}) collective-permute-start(bf16[2,225,512]{2,1,0:T(8,128)(2,1)S(1)} %collective-permute-done.refs_2_), channel_id=1, source_target_pairs={{0,32},{32,64},{64,96},{96,128},{128,160},{160,192},{192,224},{224... | collective-permute-start | bytes 1382408 | tf_op jit(solution)/shard_map/ppermute | solution.py:24
  35.8 22.2 %collective-permute-start.5 = (bf16[2,225,512]{2,1,0:T(8,128)(2,1)S(1)}, bf16[2,225,512]{2,1,0:T(8,128)(2,1)}, u32[]{:S(2)}, u32[]{:S(2)}) collective-permute-start(bf16[2,225,512]{2,1,0:T(8,128)(2,1)S(1)} %collective-permute-done.4.refs_5_), channel_id=1, source_target_pairs={{0,224},{32,0},{64,32},{96,64},{128,96},{160,128},{192,160},{224,1... | collective-permute-start | bytes 1382408 | tf_op jit(solution)/shard_map/ppermute | solution.py:24
  45.0 11.0 %collective-permute-start.14 = (bf16[64,1800]{1,0:T(8,128)(2,1)S(1)}, bf16[64,1800]{1,0:T(8,128)(2,1)S(1)}, u32[]{:S(2)}, u32[]{:S(2)}) collective-permute-start(bf16[64,1800]{1,0:T(8,128)(2,1)S(1)} %reshape.48.refs_0_), channel_id=1, source_target_pairs={{0,32},{32,64},{64,96},{96,128},{128,160},{160,192},{192,224},{224... | collective-permute-start | bytes 691208 | tf_op jit(solution)/shard_map/ppermute | solution.py:24
  46.1 19.7 %collective-permute-start.12 = (bf16[2,225,512]{2,1,0:T(8,128)(2,1)}, bf16[2,225,512]{2,1,0:T(8,128)(2,1)S(1)}, u32[]{:S(2)}, u32[]{:S(2)}) collective-permute-start(bf16[2,225,512]{2,1,0:T(8,128)(2,1)} %collective-permute-done.11.refs_4_), channel_id=1, source_target_pairs={{0,224},{32,0},{64,32},{96,64},{128,96},{160,128},{192,160},{224,1... | collective-permute-start | bytes 1382408 | tf_op jit(solution)/shard_map/ppermute | solution.py:24
  48.5 17.7 %collective-permute-start.9 = (bf16[2,225,512]{2,1,0:T(8,128)(2,1)}, bf16[2,225,512]{2,1,0:T(8,128)(2,1)S(1)}, u32[]{:S(2)}, u32[]{:S(2)}) collective-permute-start(bf16[2,225,512]{2,1,0:T(8,128)(2,1)} %collective-permute-done.8.refs_3_), channel_id=1, source_target_pairs={{0,32},{32,64},{64,96},{96,128},{128,160},{160,192},{192,224},{224... | collective-permute-start | bytes 1382408 | tf_op jit(solution)/shard_map/ppermute | solution.py:24
  56.0 9.8 %collective-permute-start.15 = (bf16[64,1800]{1,0:T(8,128)(2,1)S(1)}, bf16[64,1800]{1,0:T(8,128)(2,1)}, u32[]{:S(2)}, u32[]{:S(2)}) collective-permute-start(bf16[64,1800]{1,0:T(8,128)(2,1)S(1)} %reshape.48.refs_0_), channel_id=1, source_target_pairs={{0,224},{32,0},{64,32},{96,64},{128,96},{160,128},{192,160},{224,1... | collective-permute-start | bytes 691208 | tf_op jit(solution)/shard_map/ppermute | solution.py:24
  58.0 23.2 %collective-permute-start.2 = (bf16[2,225,512]{2,1,0:T(8,128)(2,1)}, bf16[2,225,512]{2,1,0:T(8,128)(2,1)S(1)}, u32[]{:S(2)}, u32[]{:S(2)}) collective-permute-start(bf16[2,225,512]{2,1,0:T(8,128)(2,1)} %collective-permute-done.1.refs_6_), channel_id=1, source_target_pairs={{0,32},{32,64},{64,96},{96,128},{128,160},{160,192},{192,224},{224... | collective-permute-start | bytes 1382408 | tf_op jit(solution)/shard_map/ppermute | solution.py:24
  58.0 23.2 %collective-permute-start.6 = (bf16[2,225,512]{2,1,0:T(8,128)(2,1)}, bf16[2,225,512]{2,1,0:T(8,128)(2,1)}, u32[]{:S(2)}, u32[]{:S(2)}) collective-permute-start(bf16[2,225,512]{2,1,0:T(8,128)(2,1)} %collective-permute-done.5.refs_9_), channel_id=1, source_target_pairs={{0,224},{32,0},{64,32},{96,64},{128,96},{160,128},{192,160},{224,1... | collective-permute-start | bytes 1382408 | tf_op jit(solution)/shard_map/ppermute | solution.py:24
  68.2 13.0 %collective-permute-start.16 = (bf16[64,1800]{1,0:T(8,128)(2,1)S(1)}, bf16[64,1800]{1,0:T(8,128)(2,1)}, u32[]{:S(2)}, u32[]{:S(2)}) collective-permute-start(bf16[64,1800]{1,0:T(8,128)(2,1)S(1)} %get-tuple-element.7.refs_1_), channel_id=1, source_target_pairs={{0,32},{32,64},{64,96},{96,128},{128,160},{160,192},{192,224},{224... | collective-permute-start | bytes 691208 | tf_op jit(solution)/shard_map/ppermute | solution.py:24
  71.4 9.9 %collective-permute-start.17 = (bf16[64,1800]{1,0:T(8,128)(2,1)}, bf16[64,1800]{1,0:T(8,128)(2,1)}, u32[]{:S(2)}, u32[]{:S(2)}) collective-permute-start(bf16[64,1800]{1,0:T(8,128)(2,1)} %get-tuple-element.6.refs_2_), channel_id=1, source_target_pairs={{0,224},{32,0},{64,32},{96,64},{128,96},{160,128},{192,160},{224,1... | collective-permute-start | bytes 691208 | tf_op jit(solution)/shard_map/ppermute | solution.py:24
  82.6 10.3 %collective-permute-start.18 = (bf16[64,1800]{1,0:T(8,128)(2,1)}, bf16[64,1800]{1,0:T(8,128)(2,1)S(1)}, u32[]{:S(2)}, u32[]{:S(2)}) collective-permute-start(bf16[64,1800]{1,0:T(8,128)(2,1)} %get-tuple-element.5.refs_3_), channel_id=1, source_target_pairs={{0,32},{32,64},{64,96},{96,128},{128,160},{160,192},{192,224},{224... | collective-permute-start | bytes 691208 | tf_op jit(solution)/shard_map/ppermute | solution.py:24
  85.4 22.6 %collective-permute-start.10 = (bf16[2,225,512]{2,1,0:T(8,128)(2,1)}, bf16[2,225,512]{2,1,0:T(8,128)(2,1)}, u32[]{:S(2)}, u32[]{:S(2)}) collective-permute-start(bf16[2,225,512]{2,1,0:T(8,128)(2,1)} %copy-done.2), channel_id=1, source_target_pairs={{0,32},{32,64},{64,96},{96,128},{128,160},{160,192},{192,224},{224... | collective-permute-start | bytes 1382408 | tf_op jit(solution)/shard_map/ppermute | solution.py:24
  87.2 22.5 %collective-permute-start.13 = (bf16[2,225,512]{2,1,0:T(8,128)(2,1)S(1)}, bf16[2,225,512]{2,1,0:T(8,128)(2,1)}, u32[]{:S(2)}, u32[]{:S(2)}) collective-permute-start(bf16[2,225,512]{2,1,0:T(8,128)(2,1)S(1)} %collective-permute-done.12.refs_8_), channel_id=1, source_target_pairs={{0,224},{32,0},{64,32},{96,64},{128,96},{160,128},{192,160},{224,1... | collective-permute-start | bytes 1382408 | tf_op jit(solution)/shard_map/ppermute | solution.py:24
  88.7 17.6 %collective-permute-start.19 = (bf16[64,1800]{1,0:T(8,128)(2,1)}, bf16[64,1800]{1,0:T(8,128)(2,1)S(1)}, u32[]{:S(2)}, u32[]{:S(2)}) collective-permute-start(bf16[64,1800]{1,0:T(8,128)(2,1)} %get-tuple-element.4.refs_4_), channel_id=1, source_target_pairs={{0,224},{32,0},{64,32},{96,64},{128,96},{160,128},{192,160},{224,1... | collective-permute-start | bytes 691208 | tf_op jit(solution)/shard_map/ppermute | solution.py:24
  88.8 25.3 %collective-permute-start.3 = (bf16[2,225,512]{2,1,0:T(8,128)(2,1)}, bf16[2,225,512]{2,1,0:T(8,128)(2,1)}, u32[]{:S(2)}, u32[]{:S(2)}) collective-permute-start(bf16[2,225,512]{2,1,0:T(8,128)(2,1)} %copy-done), channel_id=1, source_target_pairs={{0,32},{32,64},{64,96},{96,128},{128,160},{160,192},{192,224},{224... | collective-permute-start | bytes 1382408 | tf_op jit(solution)/shard_map/ppermute | solution.py:24
  92.9 22.5 %collective-permute-start.7 = (bf16[2,225,512]{2,1,0:T(8,128)(2,1)}, bf16[2,225,512]{2,1,0:T(8,128)(2,1)}, u32[]{:S(2)}, u32[]{:S(2)}) collective-permute-start(bf16[2,225,512]{2,1,0:T(8,128)(2,1)} %collective-permute-done.6.refs_3_), channel_id=1, source_target_pairs={{0,224},{32,0},{64,32},{96,64},{128,96},{160,128},{192,160},{224,1... | collective-permute-start | bytes 1382408 | tf_op jit(solution)/shard_map/ppermute | solution.py:24
  95.7 14.0 %copy-start.1 = (bf16[2,225,512]{2,1,0:T(8,128)(2,1)S(1)}, bf16[2,225,512]{2,1,0:T(8,128)(2,1)}, u32[]{:S(2)}) copy-start(bf16[2,225,512]{2,1,0:T(8,128)(2,1)} %copy-done) | copy-start | bytes 1382404
  106.4 12.8 %collective-permute-start.20 = (bf16[32,1800]{1,0:T(8,128)(2,1)S(1)}, bf16[32,1800]{1,0:T(8,128)(2,1)S(1)}, u32[]{:S(2)}, u32[]{:S(2)}) collective-permute-start(bf16[32,1800]{1,0:T(8,128)(2,1)S(1)} %slice.102), channel_id=1, source_target_pairs={{0,32},{32,64},{64,96},{96,128},{128,160},{160,192},{192,224},{224... | collective-permute-start | bytes 345608 | tf_op jit(solution)/shard_map/ppermute | solution.py:24
  108.0 11.1 %collective-permute-start.21 = (bf16[32,1800]{1,0:T(8,128)(2,1)S(1)}, bf16[32,1800]{1,0:T(8,128)(2,1)S(1)}, u32[]{:S(2)}, u32[]{:S(2)}) collective-permute-start(bf16[32,1800]{1,0:T(8,128)(2,1)S(1)} %slice.103), channel_id=1, source_target_pairs={{0,224},{32,0},{64,32},{96,64},{128,96},{160,128},{192,160},{224,1... | collective-permute-start | bytes 345608 | tf_op jit(solution)/shard_map/ppermute | solution.py:24
  114.0 5.1 %copy-start.4 = (bf16[64,512]{1,0:T(8,128)(2,1)S(1)}, bf16[64,512]{1,0:T(8,128)(2,1)}, u32[]{:S(2)}) copy-start(bf16[64,512]{1,0:T(8,128)(2,1)} %left_ref.1) | copy-start | bytes 196612
  114.1 5.1 %copy-start.6 = (s32[100]{0:T(128)S(1)}, s32[100]{0:T(128)}, u32[]{:S(2)}) copy-start(s32[100]{0:T(128)} %occ_ref.1) | copy-start | bytes 1204
  (3 other events, 3.2 us)
Sparse Core Ops, SparseCore 0:
  10.6 74.0 all-gather.1

commit v3 on v2

--- a/solution.py
+++ b/solution.py
@@ -14,6 +14,7 @@
 RING = 8
 QUARTERS = 4
 LANES = 256
+VLIM = 16 << 20
 OFFSETS = (0, -1, 1, -2, 2, -3, 3, 4, 4)
 UP = [(i, (i + 1) % RING) for i in range(RING)]
 DOWN = [(i, (i - 1) % RING) for i in range(RING)]
@@ -112,20 +113,15 @@
 
 
 def cycle_kernel(n, at_ref, occ_ref, low_ref, left_ref, vir_ref, *refs):
-    parts, out_ref, right, sems = refs[:n], refs[n], refs[n + 1], refs[n + 2]
+    parts, out_ref, right = refs[:n], refs[n], refs[n + 1]
     rows = left_ref.shape[0]
     each = right.shape[0] // RING
 
-    def copy(i):
+    for i in range(n):
+        size = parts[i].shape[0]
         owner = (at_ref[0] + OFFSETS[i]) & (RING - 1)
-        size = parts[i].shape[0]
         start = owner * each + (each // 2 if i == n - 1 else 0)
-        return pltpu.make_async_copy(
-            parts[i], right.at[pl.ds(pl.multiple_of(start, each // 2), size)], sems.at[i]
-        )
-
-    for i in range(n):
-        copy(i).start()
+        right[pl.ds(pl.multiple_of(start, each // 2), size), :] = parts[i][...]
     row = lax.broadcasted_iota(jnp.int32, (rows, 128), 0)
     row_label = jnp.zeros((rows, 128), jnp.int32)
     for i in range(rows // CW):
@@ -136,8 +132,6 @@
     labels = [vir_ref[...] ^ occ_ref[at_ref[1] * count + j] for j in range(count)]
     col_label = jnp.concatenate(labels, axis=1)
     allowed = ((row_label[:, :1] ^ col_label) & 7) == 0
-    for i in range(n):
-        copy(i).wait()
     total = jnp.dot(left_ref[...], right[...], preferred_element_type=jnp.float32)
     out_ref[...] = jnp.where(allowed, total, 0.0).astype(out_ref.dtype)
 
@@ -149,13 +143,9 @@
         functools.partial(cycle_kernel, len(parts)),
         out_shape=jax.ShapeDtypeStruct((rows, columns), jnp.bfloat16),
         in_specs=[scalars] * 3
-        + [WHOLE] * 2
-        + [pl.BlockSpec(memory_space=pl.ANY)] * len(parts),
+        + [WHOLE] * (2 + len(parts)),
         out_specs=WHOLE,
-        scratch_shapes=[
-            pltpu.VMEM((depth, columns), jnp.bfloat16),
-            pltpu.SemaphoreType.DMA((len(parts),)),
-        ],
+        scratch_shapes=[pltpu.VMEM((depth, columns), jnp.bfloat16)],
         compiler_params=pltpu.CompilerParams(vmem_limit_bytes=16 << 20),
         cost_estimate=pl.CostEstimate(
             flops=2 * rows * depth * columns,
@@ -209,7 +199,7 @@
     def owners(offsets):
         return (z + jnp.array(offsets, jnp.int32)) & (RING - 1)
 
-    near, middle, late = [0, -1, 1, -2, 2], [-3, 3], [4]
+    near, middle, late = [0, -1, 1], [-2, 2, -3, 3], [4]
     total = ladder_part(owners(near), gathered, blocks(near), None, False)
     regrouped[-3], regrouped[3] = (
         tie(regrouped[d], [total[:8, :128].astype(jnp.bfloat16)]) for d in (-3, 3)

time: 130 us -> 126 us (0.969)
  waiting for transfers between devices: 42.5 us -> 37.1 us
  starting transfers between devices: 44.7 us -> 48.9 us
  local copies, waits for them, and re-layouts: 6.04 us -> 4.25 us
    ppermute x22, waiting for transfers between devices: 37.7 us -> 32.3 us  [shift(): return lax.ppermute(value, 'row', UP if step > 0 else DOWN)]
    ppermute x22, starting transfers between devices: 37 us -> 41.3 us  [shift(): return lax.ppermute(value, 'row', UP if step > 0 else DOWN)]
    unnamed x22 -> x18, local copies, waits for them, and re-layouts: 1.86 us -> 0.05 us
  transfers between devices with their start and end apart: 24 -> 24, of which waited for: 9 -> 7; matrix products, arithmetic and copies ran while one was open for 4% -> 4% of each run, Pallas kernels for 12% -> 13%
where the time goes in v3:
time: 126 us
  starting transfers between devices  48.9 us (39%)
  waiting for transfers between devices  37.1 us (29%)
  Pallas kernels  18.4 us (15%)
  between operations  14.3 us (11%)
  local copies, waits for them, and re-layouts  4.25 us (3%)
  other arithmetic  2.69 us (2%)
    ppermute x22, starting transfers between devices, shift(): return lax.ppermute(value, 'row', UP if step > 0 else DOWN)  41.3 us
    ppermute x22, waiting for transfers between devices, shift(): return lax.ppermute(value, 'row', UP if step > 0 else DOWN)  32.3 us
    pallas_call x3, Pallas kernels, ladder_part(): pl.pallas_call(functools.partial(ladder_kernel, n, first, last), out_shap...  15.8 us
    all_to_all x1, starting transfers between devices, shards(): lax.all_to_all(window, ('col', 'depth'), split_axis=1, concat_axis=2, til...  7.62 us
    all_to_all x1, waiting for transfers between devices, shards(): lax.all_to_all(window, ('col', 'depth'), split_axis=1, concat_axis=2, til...  4.78 us
    dynamic_update_slice x4, other arithmetic, tie(): return lax.dynamic_update_slice(value, corner, at)  2.61 us
    pallas_call x1, Pallas kernels, cycle_part(): pl.pallas_call(functools.partial(cycle_kernel, len(parts)), out_shape=jax...  2.6 us
  transfers between devices with their start and end apart: 24, of which 7 were waited for; matrix products, arithmetic and copies ran while one was open for 4% of the time, Pallas kernels for 13%

profile of v3, /device:TPU:2, one launch (start us, length us, event | category | flops | bytes accessed | tf_op | source)
XLA Modules:
  0.0 125.7 jit_solution(16503542826175253112)
XLA Ops:
  7.2 1.9 %pad.4 = bf16[800,256]{1,0:T(8,128)(2,1)} pad(bf16[800,225]{1,0:T(8,128)(2,1)} %param.8, bf16[]{:T(256)} %constant.10.clone.1), padding=0_0x0_31 | pad | bytes 769602 | tf_op jit(solution)/shard_map/jit(_pad)/pad | solution.py:164
  9.4 2.0 %collective-permute-start = (bf16[2,225,512]{2,1,0:T(8,128)(2,1)S(1)}, bf16[2,225,512]{2,1,0:T(8,128)(2,1)S(1)}, u32[]{:S(2)}, u32[]{:S(2)}) collective-permute-start(bf16[2,225,512]{2,1,0:T(8,128)(2,1)S(1)} %reshape.43.refs_0_), channel_id=1, source_target_pairs={{0,32},{32,64},{64,96},{96,128},{128,160},{160,192},{192,224},{224... | collective-permute-start | bytes 1382408 | tf_op jit(solution)/shard_map/ppermute | solution.py:25
  11.5 4.0 %collective-permute-start.4 = (bf16[2,225,512]{2,1,0:T(8,128)(2,1)S(1)}, bf16[2,225,512]{2,1,0:T(8,128)(2,1)S(1)}, u32[]{:S(2)}, u32[]{:S(2)}) collective-permute-start(bf16[2,225,512]{2,1,0:T(8,128)(2,1)S(1)} %reshape.44.refs_1_), channel_id=1, source_target_pairs={{0,224},{32,0},{64,32},{96,64},{128,96},{160,128},{192,160},{224,1... | collective-permute-start | bytes 1382408 | tf_op jit(solution)/shard_map/ppermute | solution.py:25
  15.5 2.0 %collective-permute-start.10 = (bf16[2,225,512]{2,1,0:T(8,128)(2,1)S(1)}, bf16[2,225,512]{2,1,0:T(8,128)(2,1)}, u32[]{:S(2)}, u32[]{:S(2)}) collective-permute-start(bf16[2,225,512]{2,1,0:T(8,128)(2,1)S(1)} %reshape.43.refs_0_), channel_id=1, source_target_pairs={{0,224},{32,0},{64,32},{96,64},{128,96},{160,128},{192,160},{224,1... | collective-permute-start | bytes 1382408 | tf_op jit(solution)/shard_map/ppermute | solution.py:25
  17.7 9.3 %collective-permute-done.refs_2_ = bf16[2,225,512]{2,1,0:T(8,128)(2,1)S(1)} collective-permute-done((bf16[2,225,512]{2,1,0:T(8,128)(2,1)S(1)}, bf16[2,225,512]{2,1,0:T(8,128)(2,1)S(1)}, u32[]{:S(2)}, u32[]{:S(2)}) %collective-permute-start) | collective-permute-done | bytes 460832 | tf_op jit(solution)/shard_map/ppermute | solution.py:25
  27.0 0.9 copy.12
  27.9 7.6 %all-to-all-start = ((bf16[8,64,225]{2,0,1:T(8,128)(2,1)}), bf16[8,64,225]{2,0,1:T(8,128)(2,1)S(1)}, u32[]{:S(2)}, u32[]{:S(2)}) async-start(bf16[8,64,225]{2,0,1:T(8,128)(2,1)} %copy.12), calls=%async_computation | async-start | bytes 524288 | tf_op jit(solution)/shard_map/all_to_all | solution.py:181
  35.8 3.3 %collective-permute-start.5 = (bf16[2,225,512]{2,1,0:T(8,128)(2,1)S(1)}, bf16[2,225,512]{2,1,0:T(8,128)(2,1)}, u32[]{:S(2)}, u32[]{:S(2)}) collective-permute-start(bf16[2,225,512]{2,1,0:T(8,128)(2,1)S(1)} %collective-permute-done.4.refs_5_), channel_id=1, source_target_pairs={{0,224},{32,0},{64,32},{96,64},{128,96},{160,128},{192,160},{224,1... | collective-permute-start | bytes 1382408 | tf_op jit(solution)/shard_map/ppermute | solution.py:25
  39.2 4.8 %all-to-all-done = bf16[8,64,225]{2,0,1:T(8,128)(2,1)S(1)} async-done(((bf16[8,64,225]{2,0,1:T(8,128)(2,1)}), bf16[8,64,225]{2,0,1:T(8,128)(2,1)S(1)}, u32[]{:S(2)}, u32[]{:S(2)}) %all-to-all-start) | async-done | bytes 230432 | tf_op jit(solution)/shard_map/all_to_all | solution.py:181
  45.0 3.4 %collective-permute-start.15 = (bf16[64,1800]{1,0:T(8,128)(2,1)S(1)}, bf16[64,1800]{1,0:T(8,128)(2,1)S(1)}, u32[]{:S(2)}, u32[]{:S(2)}) collective-permute-start(bf16[64,1800]{1,0:T(8,128)(2,1)S(1)} %reshape.48.refs_0_), channel_id=1, source_target_pairs={{0,224},{32,0},{64,32},{96,64},{128,96},{160,128},{192,160},{224,1... | collective-permute-start | bytes 691208 | tf_op jit(solution)/shard_map/ppermute | solution.py:25
  48.4 1.3 %collective-permute-start.11 = (bf16[2,225,512]{2,1,0:T(8,128)(2,1)}, bf16[2,225,512]{2,1,0:T(8,128)(2,1)S(1)}, u32[]{:S(2)}, u32[]{:S(2)}) collective-permute-start(bf16[2,225,512]{2,1,0:T(8,128)(2,1)} %collective-permute-done.10.refs_4_), channel_id=1, source_target_pairs={{0,224},{32,0},{64,32},{96,64},{128,96},{160,128},{192,160},{224,1... | collective-permute-start | bytes 1382408 | tf_op jit(solution)/shard_map/ppermute | solution.py:25
  50.4 5.4 %collective-permute-done.15 = bf16[64,1800]{1,0:T(8,128)(2,1)S(1)} collective-permute-done((bf16[64,1800]{1,0:T(8,128)(2,1)S(1)}, bf16[64,1800]{1,0:T(8,128)(2,1)S(1)}, u32[]{:S(2)}, u32[]{:S(2)}) %collective-permute-start.15) | collective-permute-done | bytes 230432 | tf_op jit(solution)/shard_map/ppermute | solution.py:25
  55.8 3.3 %collective-permute-start.14 = (bf16[64,1800]{1,0:T(8,128)(2,1)S(1)}, bf16[64,1800]{1,0:T(8,128)(2,1)}, u32[]{:S(2)}, u32[]{:S(2)}) collective-permute-start(bf16[64,1800]{1,0:T(8,128)(2,1)S(1)} %reshape.48.refs_0_), channel_id=1, source_target_pairs={{0,32},{32,64},{64,96},{96,128},{128,160},{160,192},{192,224},{224... | collective-permute-start | bytes 691208 | tf_op jit(solution)/shard_map/ppermute | solution.py:25
  59.1 2.1 %collective-permute-start.2 = (bf16[2,225,512]{2,1,0:T(8,128)(2,1)}, bf16[2,225,512]{2,1,0:T(8,128)(2,1)}, u32[]{:S(2)}, u32[]{:S(2)}) collective-permute-start(bf16[2,225,512]{2,1,0:T(8,128)(2,1)} %collective-permute-done.1.refs_0_), channel_id=1, source_target_pairs={{0,32},{32,64},{64,96},{96,128},{128,160},{160,192},{192,224},{224... | collective-permute-start | bytes 1382408 | tf_op jit(solution)/shard_map/ppermute | solution.py:25
  61.2 1.2 collective-permute-start.6
  62.4 7.9 %collective-permute-done.14 = bf16[64,1800]{1,0:T(8,128)(2,1)} collective-permute-done((bf16[64,1800]{1,0:T(8,128)(2,1)S(1)}, bf16[64,1800]{1,0:T(8,128)(2,1)}, u32[]{:S(2)}, u32[]{:S(2)}) %collective-permute-start.14) | collective-permute-done | bytes 230432 | tf_op jit(solution)/shard_map/ppermute | solution.py:25
  70.3 1.3 %fusion.10 = (bf16[64,1800]{1,0:T(8,128)(2,1)S(1)}, bf16[64,1800]{1,0:T(8,128)(2,1)}) fusion(bf16[64,1800]{1,0:T(8,128)(2,1)S(1)} %collective-permute-done.15, bf16[2,225,512]{2,1,0:T(8,128)(2,1)} %collective-permute-done.9.refs_1_, bf16[2,225,512]{2,1,0:T(8,128)(2,1)S(1)} %collective-permute-done.11.refs_2_, bf16[64,1800]{1,0:T(8,128)(2,1)} %collective-permute-done.14), kind=kLoop, calls=%fused_computation.19 | loop fusion | flops 17408 | bytes 12288 | tf_op jit(solution)/shard_map/dynamic_update_slice | solution.py:35
  71.5 2.0 %collective-permute-start.16 = (bf16[64,1800]{1,0:T(8,128)(2,1)}, bf16[64,1800]{1,0:T(8,128)(2,1)}, u32[]{:S(2)}, u32[]{:S(2)}) collective-permute-start(bf16[64,1800]{1,0:T(8,128)(2,1)} %get-tuple-element.7.refs_1_), channel_id=1, source_target_pairs={{0,32},{32,64},{64,96},{96,128},{128,160},{160,192},{192,224},{224... | collective-permute-start | bytes 691208 | tf_op jit(solution)/shard_map/ppermute | solution.py:25
  73.6 1.3 %collective-permute-start.13 = (bf16[2,225,512]{2,1,0:T(8,128)(2,1)S(1)}, bf16[2,225,512]{2,1,0:T(8,128)(2,1)}, u32[]{:S(2)}, u32[]{:S(2)}) collective-permute-start(bf16[2,225,512]{2,1,0:T(8,128)(2,1)S(1)} %collective-permute-done.11.refs_2_), channel_id=1, source_target_pairs={{0,224},{32,0},{64,32},{96,64},{128,96},{160,128},{192,160},{224,1... | collective-permute-start | bytes 1382408 | tf_op jit(solution)/shard_map/ppermute | solution.py:25
  74.9 6.6 %collective-permute-done.17 = bf16[64,1800]{1,0:T(8,128)(2,1)} collective-permute-done((bf16[64,1800]{1,0:T(8,128)(2,1)S(1)}, bf16[64,1800]{1,0:T(8,128)(2,1)}, u32[]{:S(2)}, u32[]{:S(2)}) %collective-permute-start.17) | collective-permute-done | bytes 230432 | tf_op jit(solution)/shard_map/ppermute | solution.py:25
  81.5 3.3 %collective-permute-start.12 = (bf16[2,225,512]{2,1,0:T(8,128)(2,1)}, bf16[2,225,512]{2,1,0:T(8,128)(2,1)}, u32[]{:S(2)}, u32[]{:S(2)}) collective-permute-start(bf16[2,225,512]{2,1,0:T(8,128)(2,1)} %collective-permute-done.9.refs_1_), channel_id=1, source_target_pairs={{0,32},{32,64},{64,96},{96,128},{128,160},{160,192},{192,224},{224... | collective-permute-start | bytes 1382408 | tf_op jit(solution)/shard_map/ppermute | solution.py:25
  84.8 1.3 %fusion.4 = (bf16[64,1800]{1,0:T(8,128)(2,1)}, bf16[64,1800]{1,0:T(8,128)(2,1)}) fusion(bf16[64,1800]{1,0:T(8,128)(2,1)} %collective-permute-done.17, bf16[2,225,512]{2,1,0:T(8,128)(2,1)} %collective-permute-done.2.refs_4_, bf16[2,225,512]{2,1,0:T(8,128)(2,1)S(1)} %collective-permute-done.6.refs_7_, bf16[64,1800]{1,0:T(8,128)(2,1)} %collective-permute-done.16), kind=kLoop, calls=%fused_computation.9 | loop fusion | flops 17408 | bytes 12288 | tf_op jit(solution)/shard_map/dynamic_update_slice | solution.py:35
  86.4 1.8 %collective-permute-start.18 = (bf16[64,1800]{1,0:T(8,128)(2,1)}, bf16[64,1800]{1,0:T(8,128)(2,1)S(1)}, u32[]{:S(2)}, u32[]{:S(2)}) collective-permute-start(bf16[64,1800]{1,0:T(8,128)(2,1)} %get-tuple-element.5.refs_3_), channel_id=1, source_target_pairs={{0,32},{32,64},{64,96},{96,128},{128,160},{160,192},{192,224},{224... | collective-permute-start | bytes 691208 | tf_op jit(solution)/shard_map/ppermute | solution.py:25
  88.3 2.0 %collective-permute-start.3 = (bf16[2,225,512]{2,1,0:T(8,128)(2,1)}, bf16[2,225,512]{2,1,0:T(8,128)(2,1)}, u32[]{:S(2)}, u32[]{:S(2)}) collective-permute-start(bf16[2,225,512]{2,1,0:T(8,128)(2,1)} %collective-permute-done.2.refs_4_), channel_id=1, source_target_pairs={{0,32},{32,64},{64,96},{96,128},{128,160},{160,192},{192,224},{224... | collective-permute-start | bytes 1382408 | tf_op jit(solution)/shard_map/ppermute | solution.py:25
  90.3 5.4 %shard_map.95.refs_8_ = f32[800,512]{1,0:T(8,128)S(1)} custom-call(s32[3]{0:T(128)S(1)} %add_and_fusion.owner_ref, bf16[32,800,256]{2,1,0:T(8,128)(2,1)} %bitcast.36, bf16[2,225,512]{2,1,0:T(8,128)(2,1)S(1)} %reshape.43.refs_0_, bf16[2,225,512]{2,1,0:T(8,128)(2,1)S(1)} %reshape.44.refs_1_, bf16[2,225,512]{2,1,0:T(8,128)(2,1)S(1)} %collective-permute-done.refs_2_, ...), custom_call_target="tpu_custom_call" | custom-call | flops 2516582400 | bytes 8060928 | tf_op jit(solution)/shard_map/pallas_call | solution.py:98
  96.1 3.5 %collective-permute-start.7 = (bf16[2,225,512]{2,1,0:T(8,128)(2,1)S(1)}, bf16[2,225,512]{2,1,0:T(8,128)(2,1)S(1)}, u32[]{:S(2)}, u32[]{:S(2)}) collective-permute-start(bf16[2,225,512]{2,1,0:T(8,128)(2,1)S(1)} %copy-done.1), channel_id=1, source_target_pairs={{0,224},{32,0},{64,32},{96,64},{128,96},{160,128},{192,160},{224,1... | collective-permute-start | bytes 1382408 | tf_op jit(solution)/shard_map/ppermute | solution.py:25
  99.6 2.7 %collective-permute-done.18 = bf16[64,1800]{1,0:T(8,128)(2,1)S(1)} collective-permute-done((bf16[64,1800]{1,0:T(8,128)(2,1)}, bf16[64,1800]{1,0:T(8,128)(2,1)S(1)}, u32[]{:S(2)}, u32[]{:S(2)}) %collective-permute-start.18) | collective-permute-done | bytes 230432 | tf_op jit(solution)/shard_map/ppermute | solution.py:25
  102.4 1.8 %collective-permute-start.20 = (bf16[32,1800]{1,0:T(8,128)(2,1)S(1)}, bf16[32,1800]{1,0:T(8,128)(2,1)S(1)}, u32[]{:S(2)}, u32[]{:S(2)}) collective-permute-start(bf16[32,1800]{1,0:T(8,128)(2,1)S(1)} %slice.102), channel_id=1, source_target_pairs={{0,32},{32,64},{64,96},{96,128},{128,160},{160,192},{192,224},{224... | collective-permute-start | bytes 345608 | tf_op jit(solution)/shard_map/ppermute | solution.py:25
  104.2 1.5 %collective-permute-start.21 = (bf16[32,1800]{1,0:T(8,128)(2,1)S(1)}, bf16[32,1800]{1,0:T(8,128)(2,1)S(1)}, u32[]{:S(2)}, u32[]{:S(2)}) collective-permute-start(bf16[32,1800]{1,0:T(8,128)(2,1)S(1)} %slice.103), channel_id=1, source_target_pairs={{0,224},{32,0},{64,32},{96,64},{128,96},{160,128},{192,160},{224,1... | collective-permute-start | bytes 345608 | tf_op jit(solution)/shard_map/ppermute | solution.py:25
  105.7 6.9 %shard_map.96.refs_2_ = f32[800,512]{1,0:T(8,128)S(1)} custom-call(s32[4]{0:T(128)S(1)} %add_and_fusion.1.owner_ref, bf16[32,800,256]{2,1,0:T(8,128)(2,1)} %bitcast.37, bf16[2,225,512]{2,1,0:T(8,128)(2,1)} %collective-permute-done.1.refs_0_, bf16[2,225,512]{2,1,0:T(8,128)(2,1)} %collective-permute-done.9.refs_1_, ...), custom_call_target="tpu_custom_call" | custom-call | flops 3355443200 | bytes 10747904 | tf_op jit(solution)/shard_map/pallas_call | solution.py:98
  112.6 3.5 %shard_map.97 = bf16[800,512]{1,0:T(8,128)(2,1)} custom-call(s32[1]{0:T(128)S(6)} %and.12.owner_ref, bf16[32,800,256]{2,1,0:T(8,128)(2,1)} %bitcast.38, bf16[2,225,512]{2,1,0:T(8,128)(2,1)} %collective-permute-done.3.refs_0_, bf16[2,225,512]{2,1,0:T(8,128)(2,1)S(1)} %collective-permute-done.7.refs_1_, f32[800,512]{1,0:T(8,128)S(1)} %shard_map.96.refs_2_), custom_call_target="tpu_custom_call" | custom-call | flops 838860800 | bytes 2686976 | tf_op jit(solution)/shard_map/pallas_call | solution.py:98
  116.2 2.6 %shard_map.98 = bf16[64,1800]{1,0:T(8,128)(2,1)} custom-call(s32[2]{0:T(128)S(1)} %pad_add_fusion.at_ref, s32[100]{0:T(128)S(1)} %copy-done.4, s32[8]{0:T(128)S(1)} %slice.69.low_ref, bf16[64,512]{1,0:T(8,128)(2,1)S(1)} %copy-done.2, s32[1,900]{1,0:T(1,128)S(1)} %bitcast.35, bf16[64,1800]{1,0:T(8,128)(2,1)S(1)} %reshape.48.refs_0_, ...), custom_call_target="tpu_custom_call" | custom-call | flops 117964800 | bytes 2073600 | tf_op jit(solution)/shard_map/pallas_call | solution.py:142
  (60 shorter events, 3.5 us)
Async XLA Ops:
  7.2 2.0 %copy-start.6 = (bf16[900,512]{1,0:T(8,128)(2,1)S(1)}, bf16[900,512]{1,0:T(8,128)(2,1)}, u32[]{:S(2)}) copy-start(bf16[900,512]{1,0:T(8,128)(2,1)} %param.9) | copy-start | bytes 2764804
  7.2 83.1 %all-gather.2.cloned.1.call-start = ((), (), s32[]{:S(2)}) async-start(), calls=%async_computation.1 | async-start | bytes 13516800 | tf_op jit(solution)/shard_map/all_gather | solution.py:165
  9.2 8.4 %copy-start.5 = (bf16[800,225]{1,0:T(8,128)(2,1)S(1)}, bf16[800,225]{1,0:T(8,128)(2,1)}, u32[]{:S(2)}) copy-start(bf16[800,225]{1,0:T(8,128)(2,1)} %param.8) | copy-start | bytes 1080004
  9.4 17.6 %collective-permute-start = (bf16[2,225,512]{2,1,0:T(8,128)(2,1)S(1)}, bf16[2,225,512]{2,1,0:T(8,128)(2,1)S(1)}, u32[]{:S(2)}, u32[]{:S(2)}) collective-permute-start(bf16[2,225,512]{2,1,0:T(8,128)(2,1)S(1)} %reshape.43.refs_0_), channel_id=1, source_target_pairs={{0,32},{32,64},{64,96},{96,128},{128,160},{160,192},{192,224},{224... | collective-permute-start | bytes 1382408 | tf_op jit(solution)/shard_map/ppermute | solution.py:25
  11.5 15.5 %collective-permute-start.4 = (bf16[2,225,512]{2,1,0:T(8,128)(2,1)S(1)}, bf16[2,225,512]{2,1,0:T(8,128)(2,1)S(1)}, u32[]{:S(2)}, u32[]{:S(2)}) collective-permute-start(bf16[2,225,512]{2,1,0:T(8,128)(2,1)S(1)} %reshape.44.refs_1_), channel_id=1, source_target_pairs={{0,224},{32,0},{64,32},{96,64},{128,96},{160,128},{192,160},{224,1... | collective-permute-start | bytes 1382408 | tf_op jit(solution)/shard_map/ppermute | solution.py:25
  15.5 32.9 %collective-permute-start.10 = (bf16[2,225,512]{2,1,0:T(8,128)(2,1)S(1)}, bf16[2,225,512]{2,1,0:T(8,128)(2,1)}, u32[]{:S(2)}, u32[]{:S(2)}) collective-permute-start(bf16[2,225,512]{2,1,0:T(8,128)(2,1)S(1)} %reshape.43.refs_0_), channel_id=1, source_target_pairs={{0,224},{32,0},{64,32},{96,64},{128,96},{160,128},{192,160},{224,1... | collective-permute-start | bytes 1382408 | tf_op jit(solution)/shard_map/ppermute | solution.py:25
  17.5 32.1 %collective-permute-start.8 = (bf16[2,225,512]{2,1,0:T(8,128)(2,1)S(1)}, bf16[2,225,512]{2,1,0:T(8,128)(2,1)}, u32[]{:S(2)}, u32[]{:S(2)}) collective-permute-start(bf16[2,225,512]{2,1,0:T(8,128)(2,1)S(1)} %reshape.44.refs_1_), channel_id=1, source_target_pairs={{0,32},{32,64},{64,96},{96,128},{128,160},{160,192},{192,224},{224... | collective-permute-start | bytes 1382408 | tf_op jit(solution)/shard_map/ppermute | solution.py:25
  17.7 41.4 %copy-start.8 = (s32[3]{0:T(128)S(1)}, s32[3]{0:T(128)}, u32[]{:S(2)}) copy-start(s32[3]{0:T(128)} %constant.32.clone) | copy-start | bytes 40
  17.7 55.9 %copy-start.3 = (s32[900]{0:T(1024)S(1)}, s32[900]{0:T(1024)}, u32[]{:S(2)}) copy-start(s32[900]{0:T(1024)} %param.12) | copy-start | bytes 10804
  17.7 55.9 %copy-start.7 = (s32[4]{0:T(128)S(1)}, s32[4]{0:T(128)}, u32[]{:S(2)}) copy-start(s32[4]{0:T(128)} %constant.33.clone) | copy-start | bytes 52
  27.9 16.0 %all-to-all-start = ((bf16[8,64,225]{2,0,1:T(8,128)(2,1)}), bf16[8,64,225]{2,0,1:T(8,128)(2,1)S(1)}, u32[]{:S(2)}, u32[]{:S(2)}) async-start(bf16[8,64,225]{2,0,1:T(8,128)(2,1)} %copy.12), calls=%async_computation | async-start | bytes 524288 | tf_op jit(solution)/shard_map/all_to_all | solution.py:181
  35.5 23.5 %collective-permute-start.1 = (bf16[2,225,512]{2,1,0:T(8,128)(2,1)S(1)}, bf16[2,225,512]{2,1,0:T(8,128)(2,1)}, u32[]{:S(2)}, u32[]{:S(2)}) collective-permute-start(bf16[2,225,512]{2,1,0:T(8,128)(2,1)S(1)} %collective-permute-done.refs_2_), channel_id=1, source_target_pairs={{0,32},{32,64},{64,96},{96,128},{128,160},{160,192},{192,224},{224... | collective-permute-start | bytes 1382408 | tf_op jit(solution)/shard_map/ppermute | solution.py:25
  35.8 25.4 %collective-permute-start.5 = (bf16[2,225,512]{2,1,0:T(8,128)(2,1)S(1)}, bf16[2,225,512]{2,1,0:T(8,128)(2,1)}, u32[]{:S(2)}, u32[]{:S(2)}) collective-permute-start(bf16[2,225,512]{2,1,0:T(8,128)(2,1)S(1)} %collective-permute-done.4.refs_5_), channel_id=1, source_target_pairs={{0,224},{32,0},{64,32},{96,64},{128,96},{160,128},{192,160},{224,1... | collective-permute-start | bytes 1382408 | tf_op jit(solution)/shard_map/ppermute | solution.py:25
  45.0 10.8 %collective-permute-start.15 = (bf16[64,1800]{1,0:T(8,128)(2,1)S(1)}, bf16[64,1800]{1,0:T(8,128)(2,1)S(1)}, u32[]{:S(2)}, u32[]{:S(2)}) collective-permute-start(bf16[64,1800]{1,0:T(8,128)(2,1)S(1)} %reshape.48.refs_0_), channel_id=1, source_target_pairs={{0,224},{32,0},{64,32},{96,64},{128,96},{160,128},{192,160},{224,1... | collective-permute-start | bytes 691208 | tf_op jit(solution)/shard_map/ppermute | solution.py:25
  48.4 21.9 %collective-permute-start.11 = (bf16[2,225,512]{2,1,0:T(8,128)(2,1)}, bf16[2,225,512]{2,1,0:T(8,128)(2,1)S(1)}, u32[]{:S(2)}, u32[]{:S(2)}) collective-permute-start(bf16[2,225,512]{2,1,0:T(8,128)(2,1)} %collective-permute-done.10.refs_4_), channel_id=1, source_target_pairs={{0,224},{32,0},{64,32},{96,64},{128,96},{160,128},{192,160},{224,1... | collective-permute-start | bytes 1382408 | tf_op jit(solution)/shard_map/ppermute | solution.py:25
  49.7 20.6 %collective-permute-start.9 = (bf16[2,225,512]{2,1,0:T(8,128)(2,1)}, bf16[2,225,512]{2,1,0:T(8,128)(2,1)}, u32[]{:S(2)}, u32[]{:S(2)}) collective-permute-start(bf16[2,225,512]{2,1,0:T(8,128)(2,1)} %collective-permute-done.8.refs_3_), channel_id=1, source_target_pairs={{0,32},{32,64},{64,96},{96,128},{128,160},{160,192},{192,224},{224... | collective-permute-start | bytes 1382408 | tf_op jit(solution)/shard_map/ppermute | solution.py:25
  55.8 14.5 %collective-permute-start.14 = (bf16[64,1800]{1,0:T(8,128)(2,1)S(1)}, bf16[64,1800]{1,0:T(8,128)(2,1)}, u32[]{:S(2)}, u32[]{:S(2)}) collective-permute-start(bf16[64,1800]{1,0:T(8,128)(2,1)S(1)} %reshape.48.refs_0_), channel_id=1, source_target_pairs={{0,32},{32,64},{64,96},{96,128},{128,160},{160,192},{192,224},{224... | collective-permute-start | bytes 691208 | tf_op jit(solution)/shard_map/ppermute | solution.py:25
  59.1 25.7 %collective-permute-start.2 = (bf16[2,225,512]{2,1,0:T(8,128)(2,1)}, bf16[2,225,512]{2,1,0:T(8,128)(2,1)}, u32[]{:S(2)}, u32[]{:S(2)}) collective-permute-start(bf16[2,225,512]{2,1,0:T(8,128)(2,1)} %collective-permute-done.1.refs_0_), channel_id=1, source_target_pairs={{0,32},{32,64},{64,96},{96,128},{128,160},{160,192},{192,224},{224... | collective-permute-start | bytes 1382408 | tf_op jit(solution)/shard_map/ppermute | solution.py:25
  61.2 23.6 %collective-permute-start.6 = (bf16[2,225,512]{2,1,0:T(8,128)(2,1)}, bf16[2,225,512]{2,1,0:T(8,128)(2,1)S(1)}, u32[]{:S(2)}, u32[]{:S(2)}) collective-permute-start(bf16[2,225,512]{2,1,0:T(8,128)(2,1)} %collective-permute-done.5.refs_3_), channel_id=1, source_target_pairs={{0,224},{32,0},{64,32},{96,64},{128,96},{160,128},{192,160},{224,1... | collective-permute-start | bytes 1382408 | tf_op jit(solution)/shard_map/ppermute | solution.py:25
  71.5 10.0 %collective-permute-start.17 = (bf16[64,1800]{1,0:T(8,128)(2,1)S(1)}, bf16[64,1800]{1,0:T(8,128)(2,1)}, u32[]{:S(2)}, u32[]{:S(2)}) collective-permute-start(bf16[64,1800]{1,0:T(8,128)(2,1)S(1)} %get-tuple-element.6.refs_2_), channel_id=1, source_target_pairs={{0,224},{32,0},{64,32},{96,64},{128,96},{160,128},{192,160},{224,1... | collective-permute-start | bytes 691208 | tf_op jit(solution)/shard_map/ppermute | solution.py:25
  71.5 13.3 %collective-permute-start.16 = (bf16[64,1800]{1,0:T(8,128)(2,1)}, bf16[64,1800]{1,0:T(8,128)(2,1)}, u32[]{:S(2)}, u32[]{:S(2)}) collective-permute-start(bf16[64,1800]{1,0:T(8,128)(2,1)} %get-tuple-element.7.refs_1_), channel_id=1, source_target_pairs={{0,32},{32,64},{64,96},{96,128},{128,160},{160,192},{192,224},{224... | collective-permute-start | bytes 691208 | tf_op jit(solution)/shard_map/ppermute | solution.py:25
  73.6 30.6 %collective-permute-start.13 = (bf16[2,225,512]{2,1,0:T(8,128)(2,1)S(1)}, bf16[2,225,512]{2,1,0:T(8,128)(2,1)}, u32[]{:S(2)}, u32[]{:S(2)}) collective-permute-start(bf16[2,225,512]{2,1,0:T(8,128)(2,1)S(1)} %collective-permute-done.11.refs_2_), channel_id=1, source_target_pairs={{0,224},{32,0},{64,32},{96,64},{128,96},{160,128},{192,160},{224,1... | collective-permute-start | bytes 1382408 | tf_op jit(solution)/shard_map/ppermute | solution.py:25
  81.5 24.2 %collective-permute-start.12 = (bf16[2,225,512]{2,1,0:T(8,128)(2,1)}, bf16[2,225,512]{2,1,0:T(8,128)(2,1)}, u32[]{:S(2)}, u32[]{:S(2)}) collective-permute-start(bf16[2,225,512]{2,1,0:T(8,128)(2,1)} %collective-permute-done.9.refs_1_), channel_id=1, source_target_pairs={{0,32},{32,64},{64,96},{96,128},{128,160},{160,192},{192,224},{224... | collective-permute-start | bytes 1382408 | tf_op jit(solution)/shard_map/ppermute | solution.py:25
  86.2 9.9 %collective-permute-start.19 = (bf16[64,1800]{1,0:T(8,128)(2,1)}, bf16[64,1800]{1,0:T(8,128)(2,1)S(1)}, u32[]{:S(2)}, u32[]{:S(2)}) collective-permute-start(bf16[64,1800]{1,0:T(8,128)(2,1)} %get-tuple-element.4.refs_4_), channel_id=1, source_target_pairs={{0,224},{32,0},{64,32},{96,64},{128,96},{160,128},{192,160},{224,1... | collective-permute-start | bytes 691208 | tf_op jit(solution)/shard_map/ppermute | solution.py:25
  86.4 15.9 %collective-permute-start.18 = (bf16[64,1800]{1,0:T(8,128)(2,1)}, bf16[64,1800]{1,0:T(8,128)(2,1)S(1)}, u32[]{:S(2)}, u32[]{:S(2)}) collective-permute-start(bf16[64,1800]{1,0:T(8,128)(2,1)} %get-tuple-element.5.refs_3_), channel_id=1, source_target_pairs={{0,32},{32,64},{64,96},{96,128},{128,160},{160,192},{192,224},{224... | collective-permute-start | bytes 691208 | tf_op jit(solution)/shard_map/ppermute | solution.py:25
  88.3 24.3 %collective-permute-start.3 = (bf16[2,225,512]{2,1,0:T(8,128)(2,1)}, bf16[2,225,512]{2,1,0:T(8,128)(2,1)}, u32[]{:S(2)}, u32[]{:S(2)}) collective-permute-start(bf16[2,225,512]{2,1,0:T(8,128)(2,1)} %collective-permute-done.2.refs_4_), channel_id=1, source_target_pairs={{0,32},{32,64},{64,96},{96,128},{128,160},{160,192},{192,224},{224... | collective-permute-start | bytes 1382408 | tf_op jit(solution)/shard_map/ppermute | solution.py:25
  90.2 5.8 %copy-start.1 = (bf16[2,225,512]{2,1,0:T(8,128)(2,1)S(1)}, bf16[2,225,512]{2,1,0:T(8,128)(2,1)}, u32[]{:S(2)}) copy-start(bf16[2,225,512]{2,1,0:T(8,128)(2,1)} %copy-done) | copy-start | bytes 1382404
  96.1 16.5 %collective-permute-start.7 = (bf16[2,225,512]{2,1,0:T(8,128)(2,1)S(1)}, bf16[2,225,512]{2,1,0:T(8,128)(2,1)S(1)}, u32[]{:S(2)}, u32[]{:S(2)}) collective-permute-start(bf16[2,225,512]{2,1,0:T(8,128)(2,1)S(1)} %copy-done.1), channel_id=1, source_target_pairs={{0,224},{32,0},{64,32},{96,64},{128,96},{160,128},{192,160},{224,1... | collective-permute-start | bytes 1382408 | tf_op jit(solution)/shard_map/ppermute | solution.py:25
  102.4 13.8 %collective-permute-start.20 = (bf16[32,1800]{1,0:T(8,128)(2,1)S(1)}, bf16[32,1800]{1,0:T(8,128)(2,1)S(1)}, u32[]{:S(2)}, u32[]{:S(2)}) collective-permute-start(bf16[32,1800]{1,0:T(8,128)(2,1)S(1)} %slice.102), channel_id=1, source_target_pairs={{0,32},{32,64},{64,96},{96,128},{128,160},{160,192},{192,224},{224... | collective-permute-start | bytes 345608 | tf_op jit(solution)/shard_map/ppermute | solution.py:25
  104.2 12.0 %collective-permute-start.21 = (bf16[32,1800]{1,0:T(8,128)(2,1)S(1)}, bf16[32,1800]{1,0:T(8,128)(2,1)S(1)}, u32[]{:S(2)}, u32[]{:S(2)}) collective-permute-start(bf16[32,1800]{1,0:T(8,128)(2,1)S(1)} %slice.103), channel_id=1, source_target_pairs={{0,224},{32,0},{64,32},{96,64},{128,96},{160,128},{192,160},{224,1... | collective-permute-start | bytes 345608 | tf_op jit(solution)/shard_map/ppermute | solution.py:25
  112.6 3.6 %copy-start.2 = (bf16[64,512]{1,0:T(8,128)(2,1)S(1)}, bf16[64,512]{1,0:T(8,128)(2,1)}, u32[]{:S(2)}) copy-start(bf16[64,512]{1,0:T(8,128)(2,1)} %left_ref.1) | copy-start | bytes 196612
  112.6 3.6 %copy-start.4 = (s32[100]{0:T(128)S(1)}, s32[100]{0:T(128)}, u32[]{:S(2)}) copy-start(s32[100]{0:T(128)} %occ_ref.1) | copy-start | bytes 1204
  (1 other events, 1.3 us)
Sparse Core Ops, SparseCore 0:
  10.6 74.0 all-gather.1

commit v4 on v3

--- a/solution.py
+++ b/solution.py
@@ -199,7 +199,7 @@
     def owners(offsets):
         return (z + jnp.array(offsets, jnp.int32)) & (RING - 1)
 
-    near, middle, late = [0, -1, 1], [-2, 2, -3, 3], [4]
+    near, middle, late = [0, -1], [1, -2, 2, -3, 3], [4]
     total = ladder_part(owners(near), gathered, blocks(near), None, False)
     regrouped[-3], regrouped[3] = (
         tie(regrouped[d], [total[:8, :128].astype(jnp.bfloat16)]) for d in (-3, 3)

time: 126 us -> 124 us (0.984)
  starting transfers between devices: 48.9 us -> 45.2 us
  waiting for transfers between devices: 37.1 us -> 38.6 us
    ppermute x22, starting transfers between devices: 41.3 us -> 37.5 us  [shift(): return lax.ppermute(value, 'row', UP if step > 0 else DOWN)]
    ppermute x22, waiting for transfers between devices: 32.3 us -> 33.7 us  [shift(): return lax.ppermute(value, 'row', UP if step > 0 else DOWN)]
where the time goes in v4:
time: 124 us
  starting transfers between devices  45.2 us (36%)
  waiting for transfers between devices  38.6 us (31%)
  Pallas kernels  18.3 us (15%)
  between operations  14.3 us (12%)
  local copies, waits for them, and re-layouts  4.94 us (4%)
  other arithmetic  2.67 us (2%)
    ppermute x22, starting transfers between devices, shift(): return lax.ppermute(value, 'row', UP if step > 0 else DOWN)  37.5 us
    ppermute x22, waiting for transfers between devices, shift(): return lax.ppermute(value, 'row', UP if step > 0 else DOWN)  33.7 us
    pallas_call x3, Pallas kernels, ladder_part(): pl.pallas_call(functools.partial(ladder_kernel, n, first, last), out_shap...  15.8 us
    all_to_all x1, starting transfers between devices, shards(): lax.all_to_all(window, ('col', 'depth'), split_axis=1, concat_axis=2, til...  7.62 us
    all_to_all x1, waiting for transfers between devices, shards(): lax.all_to_all(window, ('col', 'depth'), split_axis=1, concat_axis=2, til...  4.79 us
    dynamic_update_slice x4, other arithmetic, tie(): return lax.dynamic_update_slice(value, corner, at)  2.58 us
  transfers between devices with their start and end apart: 24, of which 7 were waited for; matrix products, arithmetic and copies ran while one was open for 4% of the time, Pallas kernels for 13%

profile of v4, /device:TPU:2, one launch (start us, length us, event | category | flops | bytes accessed | tf_op | source)
XLA Modules:
  0.0 124.0 jit_solution(12895997535820235636)
XLA Ops:
  7.2 1.9 %pad.4 = bf16[800,256]{1,0:T(8,128)(2,1)} pad(bf16[800,225]{1,0:T(8,128)(2,1)} %param.8, bf16[]{:T(256)} %constant.11.clone.1), padding=0_0x0_31 | pad | bytes 769602 | tf_op jit(solution)/shard_map/jit(_pad)/pad | solution.py:164
  9.4 2.0 %collective-permute-start = (bf16[2,225,512]{2,1,0:T(8,128)(2,1)S(1)}, bf16[2,225,512]{2,1,0:T(8,128)(2,1)S(1)}, u32[]{:S(2)}, u32[]{:S(2)}) collective-permute-start(bf16[2,225,512]{2,1,0:T(8,128)(2,1)S(1)} %reshape.43.refs_0_), channel_id=1, source_target_pairs={{0,32},{32,64},{64,96},{96,128},{128,160},{160,192},{192,224},{224... | collective-permute-start | bytes 1382408 | tf_op jit(solution)/shard_map/ppermute | solution.py:25
  11.5 4.0 %collective-permute-start.4 = (bf16[2,225,512]{2,1,0:T(8,128)(2,1)S(1)}, bf16[2,225,512]{2,1,0:T(8,128)(2,1)S(1)}, u32[]{:S(2)}, u32[]{:S(2)}) collective-permute-start(bf16[2,225,512]{2,1,0:T(8,128)(2,1)S(1)} %reshape.44.refs_1_), channel_id=1, source_target_pairs={{0,224},{32,0},{64,32},{96,64},{128,96},{160,128},{192,160},{224,1... | collective-permute-start | bytes 1382408 | tf_op jit(solution)/shard_map/ppermute | solution.py:25
  15.5 3.2 %collective-permute-start.8 = (bf16[2,225,512]{2,1,0:T(8,128)(2,1)S(1)}, bf16[2,225,512]{2,1,0:T(8,128)(2,1)}, u32[]{:S(2)}, u32[]{:S(2)}) collective-permute-start(bf16[2,225,512]{2,1,0:T(8,128)(2,1)S(1)} %reshape.43.refs_0_), channel_id=1, source_target_pairs={{0,224},{32,0},{64,32},{96,64},{128,96},{160,128},{192,160},{224,1... | collective-permute-start | bytes 1382408 | tf_op jit(solution)/shard_map/ppermute | solution.py:25
  18.9 8.1 %collective-permute-done.refs_2_ = bf16[2,225,512]{2,1,0:T(8,128)(2,1)S(1)} collective-permute-done((bf16[2,225,512]{2,1,0:T(8,128)(2,1)S(1)}, bf16[2,225,512]{2,1,0:T(8,128)(2,1)S(1)}, u32[]{:S(2)}, u32[]{:S(2)}) %collective-permute-start) | collective-permute-done | bytes 460832 | tf_op jit(solution)/shard_map/ppermute | solution.py:25
  27.9 7.6 %all-to-all-start = ((bf16[8,64,225]{2,0,1:T(8,128)(2,1)}), bf16[8,64,225]{2,0,1:T(8,128)(2,1)S(1)}, u32[]{:S(2)}, u32[]{:S(2)}) async-start(bf16[8,64,225]{2,0,1:T(8,128)(2,1)} %copy.12), calls=%async_computation | async-start | bytes 524288 | tf_op jit(solution)/shard_map/all_to_all | solution.py:181
  35.8 3.3 %collective-permute-start.5 = (bf16[2,225,512]{2,1,0:T(8,128)(2,1)S(1)}, bf16[2,225,512]{2,1,0:T(8,128)(2,1)}, u32[]{:S(2)}, u32[]{:S(2)}) collective-permute-start(bf16[2,225,512]{2,1,0:T(8,128)(2,1)S(1)} %collective-permute-done.4.refs_1_), channel_id=1, source_target_pairs={{0,224},{32,0},{64,32},{96,64},{128,96},{160,128},{192,160},{224,1... | collective-permute-start | bytes 1382408 | tf_op jit(solution)/shard_map/ppermute | solution.py:25
  39.2 4.8 %all-to-all-done = bf16[8,64,225]{2,0,1:T(8,128)(2,1)S(1)} async-done(((bf16[8,64,225]{2,0,1:T(8,128)(2,1)}), bf16[8,64,225]{2,0,1:T(8,128)(2,1)S(1)}, u32[]{:S(2)}, u32[]{:S(2)}) %all-to-all-start) | async-done | bytes 230432 | tf_op jit(solution)/shard_map/all_to_all | solution.py:181
  45.0 1.2 collective-permute-start.14
  46.1 2.1 %collective-permute-start.10 = (bf16[2,225,512]{2,1,0:T(8,128)(2,1)}, bf16[2,225,512]{2,1,0:T(8,128)(2,1)S(1)}, u32[]{:S(2)}, u32[]{:S(2)}) collective-permute-start(bf16[2,225,512]{2,1,0:T(8,128)(2,1)} %collective-permute-done.9.refs_3_), channel_id=1, source_target_pairs={{0,32},{32,64},{64,96},{96,128},{128,160},{160,192},{192,224},{224... | collective-permute-start | bytes 1382408 | tf_op jit(solution)/shard_map/ppermute | solution.py:25
  48.3 1.1 collective-permute-start.11
  49.4 6.6 %collective-permute-done.14 = bf16[64,1800]{1,0:T(8,128)(2,1)S(1)} collective-permute-done((bf16[64,1800]{1,0:T(8,128)(2,1)S(1)}, bf16[64,1800]{1,0:T(8,128)(2,1)S(1)}, u32[]{:S(2)}, u32[]{:S(2)}) %collective-permute-start.14) | collective-permute-done | bytes 230432 | tf_op jit(solution)/shard_map/ppermute | solution.py:25
  56.0 2.1 %collective-permute-start.15 = (bf16[64,1800]{1,0:T(8,128)(2,1)S(1)}, bf16[64,1800]{1,0:T(8,128)(2,1)}, u32[]{:S(2)}, u32[]{:S(2)}) collective-permute-start(bf16[64,1800]{1,0:T(8,128)(2,1)S(1)} %reshape.48.refs_0_), channel_id=1, source_target_pairs={{0,224},{32,0},{64,32},{96,64},{128,96},{160,128},{192,160},{224,1... | collective-permute-start | bytes 691208 | tf_op jit(solution)/shard_map/ppermute | solution.py:25
  58.1 3.2 %collective-permute-start.6 = (bf16[2,225,512]{2,1,0:T(8,128)(2,1)}, bf16[2,225,512]{2,1,0:T(8,128)(2,1)}, u32[]{:S(2)}, u32[]{:S(2)}) collective-permute-start(bf16[2,225,512]{2,1,0:T(8,128)(2,1)} %collective-permute-done.5.refs_5_), channel_id=1, source_target_pairs={{0,224},{32,0},{64,32},{96,64},{128,96},{160,128},{192,160},{224,1... | collective-permute-start | bytes 1382408 | tf_op jit(solution)/shard_map/ppermute | solution.py:25
  61.3 7.0 %collective-permute-done.15 = bf16[64,1800]{1,0:T(8,128)(2,1)} collective-permute-done((bf16[64,1800]{1,0:T(8,128)(2,1)S(1)}, bf16[64,1800]{1,0:T(8,128)(2,1)}, u32[]{:S(2)}, u32[]{:S(2)}) %collective-permute-start.15) | collective-permute-done | bytes 230432 | tf_op jit(solution)/shard_map/ppermute | solution.py:25
  68.3 1.3 %fusion.10 = (bf16[64,1800]{1,0:T(8,128)(2,1)}, bf16[64,1800]{1,0:T(8,128)(2,1)S(1)}) fusion(bf16[64,1800]{1,0:T(8,128)(2,1)} %collective-permute-done.15, bf16[2,225,512]{2,1,0:T(8,128)(2,1)S(1)} %collective-permute-done.10.refs_3_, bf16[2,225,512]{2,1,0:T(8,128)(2,1)} %collective-permute-done.11.refs_4_, bf16[64,1800]{1,0:T(8,128)(2,1)S(1)} %collective-permute-done.14), kind=kLoop, calls=%fused_computation.19 | loop fusion | flops 17408 | bytes 12288 | tf_op jit(solution)/shard_map/dynamic_update_slice | solution.py:35
  70.3 2.1 %collective-permute-start.16 = (bf16[64,1800]{1,0:T(8,128)(2,1)}, bf16[64,1800]{1,0:T(8,128)(2,1)S(1)}, u32[]{:S(2)}, u32[]{:S(2)}) collective-permute-start(bf16[64,1800]{1,0:T(8,128)(2,1)} %copy-done.2), channel_id=1, source_target_pairs={{0,32},{32,64},{64,96},{96,128},{128,160},{160,192},{192,224},{224... | collective-permute-start | bytes 691208 | tf_op jit(solution)/shard_map/ppermute | solution.py:25
  72.4 1.2 collective-permute-start.17
  73.6 0.9 collective-permute-start.12
  74.5 7.1 %collective-permute-done.16 = bf16[64,1800]{1,0:T(8,128)(2,1)S(1)} collective-permute-done((bf16[64,1800]{1,0:T(8,128)(2,1)}, bf16[64,1800]{1,0:T(8,128)(2,1)S(1)}, u32[]{:S(2)}, u32[]{:S(2)}) %collective-permute-start.16) | collective-permute-done | bytes 230432 | tf_op jit(solution)/shard_map/ppermute | solution.py:25
  81.6 2.1 %collective-permute-start.13 = (bf16[2,225,512]{2,1,0:T(8,128)(2,1)}, bf16[2,225,512]{2,1,0:T(8,128)(2,1)}, u32[]{:S(2)}, u32[]{:S(2)}) collective-permute-start(bf16[2,225,512]{2,1,0:T(8,128)(2,1)} %collective-permute-done.11.refs_4_), channel_id=1, source_target_pairs={{0,224},{32,0},{64,32},{96,64},{128,96},{160,128},{192,160},{224,1... | collective-permute-start | bytes 1382408 | tf_op jit(solution)/shard_map/ppermute | solution.py:25
  83.7 1.3 %fusion.4 = (bf16[64,1800]{1,0:T(8,128)(2,1)}, bf16[64,1800]{1,0:T(8,128)(2,1)S(1)}) fusion(bf16[64,1800]{1,0:T(8,128)(2,1)} %collective-permute-done.17, bf16[2,225,512]{2,1,0:T(8,128)(2,1)S(1)} %collective-permute-done.2.refs_6_, bf16[2,225,512]{2,1,0:T(8,128)(2,1)} %collective-permute-done.6.refs_9_, bf16[64,1800]{1,0:T(8,128)(2,1)S(1)} %collective-permute-done.16), kind=kLoop, calls=%fused_computation.9 | loop fusion | flops 17408 | bytes 12288 | tf_op jit(solution)/shard_map/dynamic_update_slice | solution.py:35
  85.0 0.9 collective-permute-start.18
  85.9 2.3 %collective-permute-start.19 = (bf16[64,1800]{1,0:T(8,128)(2,1)}, bf16[64,1800]{1,0:T(8,128)(2,1)S(1)}, u32[]{:S(2)}, u32[]{:S(2)}) collective-permute-start(bf16[64,1800]{1,0:T(8,128)(2,1)} %get-tuple-element.4.refs_4_), channel_id=1, source_target_pairs={{0,224},{32,0},{64,32},{96,64},{128,96},{160,128},{192,160},{224,1... | collective-permute-start | bytes 691208 | tf_op jit(solution)/shard_map/ppermute | solution.py:25
  88.4 3.9 %shard_map.95.refs_10_ = f32[800,512]{1,0:T(8,128)S(1)} custom-call(s32[2]{0:T(128)S(1)} %add_and_fusion.owner_ref, bf16[32,800,256]{2,1,0:T(8,128)(2,1)} %bitcast.36, bf16[2,225,512]{2,1,0:T(8,128)(2,1)S(1)} %reshape.43.refs_0_, bf16[2,225,512]{2,1,0:T(8,128)(2,1)S(1)} %reshape.44.refs_1_, bf16[2,225,512]{2,1,0:T(8,128)(2,1)S(1)} %collective-permute-done.refs_2_, ...), custom_call_target="tpu_custom_call" | custom-call | flops 1677721600 | bytes 5373952 | tf_op jit(solution)/shard_map/pallas_call | solution.py:98
  92.3 4.8 %collective-permute-done.18 = bf16[64,1800]{1,0:T(8,128)(2,1)S(1)} collective-permute-done((bf16[64,1800]{1,0:T(8,128)(2,1)S(1)}, bf16[64,1800]{1,0:T(8,128)(2,1)S(1)}, u32[]{:S(2)}, u32[]{:S(2)}) %collective-permute-start.18) | collective-permute-done | bytes 230432 | tf_op jit(solution)/shard_map/ppermute | solution.py:25
  97.1 2.1 %collective-permute-start.7 = (bf16[2,225,512]{2,1,0:T(8,128)(2,1)}, bf16[2,225,512]{2,1,0:T(8,128)(2,1)S(1)}, u32[]{:S(2)}, u32[]{:S(2)}) collective-permute-start(bf16[2,225,512]{2,1,0:T(8,128)(2,1)} %collective-permute-done.6.refs_9_), channel_id=1, source_target_pairs={{0,224},{32,0},{64,32},{96,64},{128,96},{160,128},{192,160},{224,1... | collective-permute-start | bytes 1382408 | tf_op jit(solution)/shard_map/ppermute | solution.py:25
  99.2 1.0 collective-permute-start.20
  100.2 2.4 %collective-permute-start.21 = (bf16[32,1800]{1,0:T(8,128)(2,1)S(1)}, bf16[32,1800]{1,0:T(8,128)(2,1)S(1)}, u32[]{:S(2)}, u32[]{:S(2)}) collective-permute-start(bf16[32,1800]{1,0:T(8,128)(2,1)S(1)} %slice.103), channel_id=1, source_target_pairs={{0,224},{32,0},{64,32},{96,64},{128,96},{160,128},{192,160},{224,1... | collective-permute-start | bytes 345608 | tf_op jit(solution)/shard_map/ppermute | solution.py:25
  102.6 8.3 %shard_map.96.refs_2_ = f32[800,512]{1,0:T(8,128)S(1)} custom-call(s32[5]{0:T(128)S(1)} %add_and_fusion.1.owner_ref, bf16[32,800,256]{2,1,0:T(8,128)(2,1)} %bitcast.37, bf16[2,225,512]{2,1,0:T(8,128)(2,1)} %collective-permute-done.8.refs_0_, bf16[2,225,512]{2,1,0:T(8,128)(2,1)S(1)} %collective-permute-done.4.refs_1_, ...), custom_call_target="tpu_custom_call" | custom-call | flops 4194304000 | bytes 13434880 | tf_op jit(solution)/shard_map/pallas_call | solution.py:98
  111.0 3.6 %shard_map.97 = bf16[800,512]{1,0:T(8,128)(2,1)} custom-call(s32[1]{0:T(128)S(6)} %and.12.owner_ref, bf16[32,800,256]{2,1,0:T(8,128)(2,1)} %bitcast.38, bf16[2,225,512]{2,1,0:T(8,128)(2,1)} %collective-permute-done.3.refs_0_, bf16[2,225,512]{2,1,0:T(8,128)(2,1)S(1)} %collective-permute-done.7.refs_1_, f32[800,512]{1,0:T(8,128)S(1)} %shard_map.96.refs_2_), custom_call_target="tpu_custom_call" | custom-call | flops 838860800 | bytes 2686976 | tf_op jit(solution)/shard_map/pallas_call | solution.py:98
  114.6 2.5 %shard_map.98 = bf16[64,1800]{1,0:T(8,128)(2,1)} custom-call(s32[2]{0:T(128)S(1)} %pad_add_fusion.at_ref, s32[100]{0:T(128)S(1)} %copy-done.6, s32[8]{0:T(128)S(1)} %slice.69.low_ref, bf16[64,512]{1,0:T(8,128)(2,1)S(1)} %copy-done.4, s32[1,900]{1,0:T(1,128)S(1)} %bitcast.35, bf16[64,1800]{1,0:T(8,128)(2,1)S(1)} %reshape.48.refs_0_, ...), custom_call_target="tpu_custom_call" | custom-call | flops 117964800 | bytes 2073600 | tf_op jit(solution)/shard_map/pallas_call | solution.py:142
  (62 shorter events, 3.6 us)
Async XLA Ops:
  7.2 2.0 %copy-start.8 = (bf16[900,512]{1,0:T(8,128)(2,1)S(1)}, bf16[900,512]{1,0:T(8,128)(2,1)}, u32[]{:S(2)}) copy-start(bf16[900,512]{1,0:T(8,128)(2,1)} %param.9) | copy-start | bytes 2764804
  7.2 81.2 %all-gather.2.cloned.1.call-start = ((), (), s32[]{:S(2)}) async-start(), calls=%async_computation.1 | async-start | bytes 13516800 | tf_op jit(solution)/shard_map/all_gather | solution.py:165
  9.2 9.6 %copy-start.7 = (bf16[800,225]{1,0:T(8,128)(2,1)S(1)}, bf16[800,225]{1,0:T(8,128)(2,1)}, u32[]{:S(2)}) copy-start(bf16[800,225]{1,0:T(8,128)(2,1)} %param.8) | copy-start | bytes 1080004
  9.4 17.6 %collective-permute-start = (bf16[2,225,512]{2,1,0:T(8,128)(2,1)S(1)}, bf16[2,225,512]{2,1,0:T(8,128)(2,1)S(1)}, u32[]{:S(2)}, u32[]{:S(2)}) collective-permute-start(bf16[2,225,512]{2,1,0:T(8,128)(2,1)S(1)} %reshape.43.refs_0_), channel_id=1, source_target_pairs={{0,32},{32,64},{64,96},{96,128},{128,160},{160,192},{192,224},{224... | collective-permute-start | bytes 1382408 | tf_op jit(solution)/shard_map/ppermute | solution.py:25
  11.5 15.5 %collective-permute-start.4 = (bf16[2,225,512]{2,1,0:T(8,128)(2,1)S(1)}, bf16[2,225,512]{2,1,0:T(8,128)(2,1)S(1)}, u32[]{:S(2)}, u32[]{:S(2)}) collective-permute-start(bf16[2,225,512]{2,1,0:T(8,128)(2,1)S(1)} %reshape.44.refs_1_), channel_id=1, source_target_pairs={{0,224},{32,0},{64,32},{96,64},{128,96},{160,128},{192,160},{224,1... | collective-permute-start | bytes 1382408 | tf_op jit(solution)/shard_map/ppermute | solution.py:25
  15.5 30.6 %collective-permute-start.9 = (bf16[2,225,512]{2,1,0:T(8,128)(2,1)S(1)}, bf16[2,225,512]{2,1,0:T(8,128)(2,1)}, u32[]{:S(2)}, u32[]{:S(2)}) collective-permute-start(bf16[2,225,512]{2,1,0:T(8,128)(2,1)S(1)} %reshape.44.refs_1_), channel_id=1, source_target_pairs={{0,32},{32,64},{64,96},{96,128},{128,160},{160,192},{192,224},{224... | collective-permute-start | bytes 1382408 | tf_op jit(solution)/shard_map/ppermute | solution.py:25
  15.5 32.7 %collective-permute-start.8 = (bf16[2,225,512]{2,1,0:T(8,128)(2,1)S(1)}, bf16[2,225,512]{2,1,0:T(8,128)(2,1)}, u32[]{:S(2)}, u32[]{:S(2)}) collective-permute-start(bf16[2,225,512]{2,1,0:T(8,128)(2,1)S(1)} %reshape.43.refs_0_), channel_id=1, source_target_pairs={{0,224},{32,0},{64,32},{96,64},{128,96},{160,128},{192,160},{224,1... | collective-permute-start | bytes 1382408 | tf_op jit(solution)/shard_map/ppermute | solution.py:25
  18.9 54.7 %copy-start.5 = (s32[900]{0:T(1024)S(1)}, s32[900]{0:T(1024)}, u32[]{:S(2)}) copy-start(s32[900]{0:T(1024)} %param.12) | copy-start | bytes 10804
  18.9 54.7 %copy-start.9 = (s32[5]{0:T(128)S(1)}, s32[5]{0:T(128)}, u32[]{:S(2)}) copy-start(s32[5]{0:T(128)} %constant.34.clone) | copy-start | bytes 64
  27.9 16.0 %all-to-all-start = ((bf16[8,64,225]{2,0,1:T(8,128)(2,1)}), bf16[8,64,225]{2,0,1:T(8,128)(2,1)S(1)}, u32[]{:S(2)}, u32[]{:S(2)}) async-start(bf16[8,64,225]{2,0,1:T(8,128)(2,1)} %copy.12), calls=%async_computation | async-start | bytes 524288 | tf_op jit(solution)/shard_map/all_to_all | solution.py:181
  35.5 22.5 %collective-permute-start.1 = (bf16[2,225,512]{2,1,0:T(8,128)(2,1)S(1)}, bf16[2,225,512]{2,1,0:T(8,128)(2,1)}, u32[]{:S(2)}, u32[]{:S(2)}) collective-permute-start(bf16[2,225,512]{2,1,0:T(8,128)(2,1)S(1)} %collective-permute-done.refs_2_), channel_id=1, source_target_pairs={{0,32},{32,64},{64,96},{96,128},{128,160},{160,192},{192,224},{224... | collective-permute-start | bytes 1382408 | tf_op jit(solution)/shard_map/ppermute | solution.py:25
  35.8 22.2 %collective-permute-start.5 = (bf16[2,225,512]{2,1,0:T(8,128)(2,1)S(1)}, bf16[2,225,512]{2,1,0:T(8,128)(2,1)}, u32[]{:S(2)}, u32[]{:S(2)}) collective-permute-start(bf16[2,225,512]{2,1,0:T(8,128)(2,1)S(1)} %collective-permute-done.4.refs_1_), channel_id=1, source_target_pairs={{0,224},{32,0},{64,32},{96,64},{128,96},{160,128},{192,160},{224,1... | collective-permute-start | bytes 1382408 | tf_op jit(solution)/shard_map/ppermute | solution.py:25
  45.0 11.0 %collective-permute-start.14 = (bf16[64,1800]{1,0:T(8,128)(2,1)S(1)}, bf16[64,1800]{1,0:T(8,128)(2,1)S(1)}, u32[]{:S(2)}, u32[]{:S(2)}) collective-permute-start(bf16[64,1800]{1,0:T(8,128)(2,1)S(1)} %reshape.48.refs_0_), channel_id=1, source_target_pairs={{0,32},{32,64},{64,96},{96,128},{128,160},{160,192},{192,224},{224... | collective-permute-start | bytes 691208 | tf_op jit(solution)/shard_map/ppermute | solution.py:25
  46.1 22.2 %collective-permute-start.10 = (bf16[2,225,512]{2,1,0:T(8,128)(2,1)}, bf16[2,225,512]{2,1,0:T(8,128)(2,1)S(1)}, u32[]{:S(2)}, u32[]{:S(2)}) collective-permute-start(bf16[2,225,512]{2,1,0:T(8,128)(2,1)} %collective-permute-done.9.refs_3_), channel_id=1, source_target_pairs={{0,32},{32,64},{64,96},{96,128},{128,160},{160,192},{192,224},{224... | collective-permute-start | bytes 1382408 | tf_op jit(solution)/shard_map/ppermute | solution.py:25
  48.3 20.1 %collective-permute-start.11 = (bf16[2,225,512]{2,1,0:T(8,128)(2,1)}, bf16[2,225,512]{2,1,0:T(8,128)(2,1)}, u32[]{:S(2)}, u32[]{:S(2)}) collective-permute-start(bf16[2,225,512]{2,1,0:T(8,128)(2,1)} %collective-permute-done.8.refs_0_), channel_id=1, source_target_pairs={{0,224},{32,0},{64,32},{96,64},{128,96},{160,128},{192,160},{224,1... | collective-permute-start | bytes 1382408 | tf_op jit(solution)/shard_map/ppermute | solution.py:25
  56.0 12.3 %collective-permute-start.15 = (bf16[64,1800]{1,0:T(8,128)(2,1)S(1)}, bf16[64,1800]{1,0:T(8,128)(2,1)}, u32[]{:S(2)}, u32[]{:S(2)}) collective-permute-start(bf16[64,1800]{1,0:T(8,128)(2,1)S(1)} %reshape.48.refs_0_), channel_id=1, source_target_pairs={{0,224},{32,0},{64,32},{96,64},{128,96},{160,128},{192,160},{224,1... | collective-permute-start | bytes 691208 | tf_op jit(solution)/shard_map/ppermute | solution.py:25
  58.0 25.6 %collective-permute-start.2 = (bf16[2,225,512]{2,1,0:T(8,128)(2,1)}, bf16[2,225,512]{2,1,0:T(8,128)(2,1)S(1)}, u32[]{:S(2)}, u32[]{:S(2)}) collective-permute-start(bf16[2,225,512]{2,1,0:T(8,128)(2,1)} %collective-permute-done.1.refs_2_), channel_id=1, source_target_pairs={{0,32},{32,64},{64,96},{96,128},{128,160},{160,192},{192,224},{224... | collective-permute-start | bytes 1382408 | tf_op jit(solution)/shard_map/ppermute | solution.py:25
  58.1 25.6 %collective-permute-start.6 = (bf16[2,225,512]{2,1,0:T(8,128)(2,1)}, bf16[2,225,512]{2,1,0:T(8,128)(2,1)}, u32[]{:S(2)}, u32[]{:S(2)}) collective-permute-start(bf16[2,225,512]{2,1,0:T(8,128)(2,1)} %collective-permute-done.5.refs_5_), channel_id=1, source_target_pairs={{0,224},{32,0},{64,32},{96,64},{128,96},{160,128},{192,160},{224,1... | collective-permute-start | bytes 1382408 | tf_op jit(solution)/shard_map/ppermute | solution.py:25
  70.3 11.3 %collective-permute-start.16 = (bf16[64,1800]{1,0:T(8,128)(2,1)}, bf16[64,1800]{1,0:T(8,128)(2,1)S(1)}, u32[]{:S(2)}, u32[]{:S(2)}) collective-permute-start(bf16[64,1800]{1,0:T(8,128)(2,1)} %copy-done.2), channel_id=1, source_target_pairs={{0,32},{32,64},{64,96},{96,128},{128,160},{160,192},{192,224},{224... | collective-permute-start | bytes 691208 | tf_op jit(solution)/shard_map/ppermute | solution.py:25
  72.4 11.3 %collective-permute-start.17 = (bf16[64,1800]{1,0:T(8,128)(2,1)}, bf16[64,1800]{1,0:T(8,128)(2,1)}, u32[]{:S(2)}, u32[]{:S(2)}) collective-permute-start(bf16[64,1800]{1,0:T(8,128)(2,1)} %get-tuple-element.6.refs_2_), channel_id=1, source_target_pairs={{0,224},{32,0},{64,32},{96,64},{128,96},{160,128},{192,160},{224,1... | collective-permute-start | bytes 691208 | tf_op jit(solution)/shard_map/ppermute | solution.py:25
  73.6 26.6 %collective-permute-start.12 = (bf16[2,225,512]{2,1,0:T(8,128)(2,1)S(1)}, bf16[2,225,512]{2,1,0:T(8,128)(2,1)}, u32[]{:S(2)}, u32[]{:S(2)}) collective-permute-start(bf16[2,225,512]{2,1,0:T(8,128)(2,1)S(1)} %collective-permute-done.10.refs_3_), channel_id=1, source_target_pairs={{0,32},{32,64},{64,96},{96,128},{128,160},{160,192},{192,224},{224... | collective-permute-start | bytes 1382408 | tf_op jit(solution)/shard_map/ppermute | solution.py:25
  81.6 21.0 %collective-permute-start.13 = (bf16[2,225,512]{2,1,0:T(8,128)(2,1)}, bf16[2,225,512]{2,1,0:T(8,128)(2,1)}, u32[]{:S(2)}, u32[]{:S(2)}) collective-permute-start(bf16[2,225,512]{2,1,0:T(8,128)(2,1)} %collective-permute-done.11.refs_4_), channel_id=1, source_target_pairs={{0,224},{32,0},{64,32},{96,64},{128,96},{160,128},{192,160},{224,1... | collective-permute-start | bytes 1382408 | tf_op jit(solution)/shard_map/ppermute | solution.py:25
  85.0 12.1 %collective-permute-start.18 = (bf16[64,1800]{1,0:T(8,128)(2,1)S(1)}, bf16[64,1800]{1,0:T(8,128)(2,1)S(1)}, u32[]{:S(2)}, u32[]{:S(2)}) collective-permute-start(bf16[64,1800]{1,0:T(8,128)(2,1)S(1)} %get-tuple-element.5.refs_3_), channel_id=1, source_target_pairs={{0,32},{32,64},{64,96},{96,128},{128,160},{160,192},{192,224},{224... | collective-permute-start | bytes 691208 | tf_op jit(solution)/shard_map/ppermute | solution.py:25
  85.9 13.2 %collective-permute-start.19 = (bf16[64,1800]{1,0:T(8,128)(2,1)}, bf16[64,1800]{1,0:T(8,128)(2,1)S(1)}, u32[]{:S(2)}, u32[]{:S(2)}) collective-permute-start(bf16[64,1800]{1,0:T(8,128)(2,1)} %get-tuple-element.4.refs_4_), channel_id=1, source_target_pairs={{0,224},{32,0},{64,32},{96,64},{128,96},{160,128},{192,160},{224,1... | collective-permute-start | bytes 691208 | tf_op jit(solution)/shard_map/ppermute | solution.py:25
  88.3 22.6 %collective-permute-start.3 = (bf16[2,225,512]{2,1,0:T(8,128)(2,1)}, bf16[2,225,512]{2,1,0:T(8,128)(2,1)}, u32[]{:S(2)}, u32[]{:S(2)}) collective-permute-start(bf16[2,225,512]{2,1,0:T(8,128)(2,1)} %copy-done), channel_id=1, source_target_pairs={{0,32},{32,64},{64,96},{96,128},{128,160},{160,192},{192,224},{224... | collective-permute-start | bytes 1382408 | tf_op jit(solution)/shard_map/ppermute | solution.py:25
  88.3 14.3 %copy-start.1 = (bf16[2,225,512]{2,1,0:T(8,128)(2,1)S(1)}, bf16[2,225,512]{2,1,0:T(8,128)(2,1)}, u32[]{:S(2)}) copy-start(bf16[2,225,512]{2,1,0:T(8,128)(2,1)} %copy-done) | copy-start | bytes 1382404
  97.1 13.9 %collective-permute-start.7 = (bf16[2,225,512]{2,1,0:T(8,128)(2,1)}, bf16[2,225,512]{2,1,0:T(8,128)(2,1)S(1)}, u32[]{:S(2)}, u32[]{:S(2)}) collective-permute-start(bf16[2,225,512]{2,1,0:T(8,128)(2,1)} %collective-permute-done.6.refs_9_), channel_id=1, source_target_pairs={{0,224},{32,0},{64,32},{96,64},{128,96},{160,128},{192,160},{224,1... | collective-permute-start | bytes 1382408 | tf_op jit(solution)/shard_map/ppermute | solution.py:25
  99.2 15.4 %collective-permute-start.20 = (bf16[32,1800]{1,0:T(8,128)(2,1)S(1)}, bf16[32,1800]{1,0:T(8,128)(2,1)S(1)}, u32[]{:S(2)}, u32[]{:S(2)}) collective-permute-start(bf16[32,1800]{1,0:T(8,128)(2,1)S(1)} %slice.102), channel_id=1, source_target_pairs={{0,32},{32,64},{64,96},{96,128},{128,160},{160,192},{192,224},{224... | collective-permute-start | bytes 345608 | tf_op jit(solution)/shard_map/ppermute | solution.py:25
  100.2 14.4 %collective-permute-start.21 = (bf16[32,1800]{1,0:T(8,128)(2,1)S(1)}, bf16[32,1800]{1,0:T(8,128)(2,1)S(1)}, u32[]{:S(2)}, u32[]{:S(2)}) collective-permute-start(bf16[32,1800]{1,0:T(8,128)(2,1)S(1)} %slice.103), channel_id=1, source_target_pairs={{0,224},{32,0},{64,32},{96,64},{128,96},{160,128},{192,160},{224,1... | collective-permute-start | bytes 345608 | tf_op jit(solution)/shard_map/ppermute | solution.py:25
  110.9 3.7 %copy-start.3 = (bf16[64,1800]{1,0:T(8,128)(2,1)S(1)}, bf16[64,1800]{1,0:T(8,128)(2,1)}, u32[]{:S(2)}) copy-start(bf16[64,1800]{1,0:T(8,128)(2,1)} %copy-done.2) | copy-start | bytes 691204
  110.9 3.7 %copy-start.4 = (bf16[64,512]{1,0:T(8,128)(2,1)S(1)}, bf16[64,512]{1,0:T(8,128)(2,1)}, u32[]{:S(2)}) copy-start(bf16[64,512]{1,0:T(8,128)(2,1)} %left_ref.1) | copy-start | bytes 196612
  110.9 3.7 %copy-start.6 = (s32[100]{0:T(128)S(1)}, s32[100]{0:T(128)}, u32[]{:S(2)}) copy-start(s32[100]{0:T(128)} %occ_ref.1) | copy-start | bytes 1204
  (2 other events, 2.0 us)
Sparse Core Ops, SparseCore 0:
  10.6 74.0 all-gather.1
